TPU v7x, 32 devices: a whole 2x2x4 slice. The times are simulated.
32 devices in a mesh: grp: 2 (over y), seq: 4 (over z), req: 2 (over x), hd: 2 (over core).
Axes of the slice: x: 2, y: 2, z: 4, core: 2. Of those that a mesh axis runs over, the one named last changes fastest.
Arguments:
- cache: bfloat16 [8, 8, 1536, 256], P(('grp', 'req'), 'hd', 'seq'), parts along dimension 0, may hold values from -7 to 7
- evicted: bfloat16 [8, 8, 256, 256], P(('grp', 'req'), 'hd', 'seq'), parts along dimension 0, may hold values from -6 to 6
- merge_weight: bfloat16 [8, 8, 256], P(('grp', 'req'), 'hd', 'seq'), parts along dimension 0, may hold values from 0.25 to 2.5
- targets: int32 [8, 8, 256], P(('grp', 'req'), 'hd', 'seq'), parts along dimension 0, may hold values from 0 to 1535, as said below
- kept_counts: int32 [8, 4], P(('grp', 'req'), 'seq'), parts along dimension 0, may hold values from 192 to 384, as said below
- queries: bfloat16 [4, 8, 64, 128], P(None, ('grp', 'req'), 'hd'), parts along dimension 1, may hold values from -1024 to 1024
- new_rows: bfloat16 [4, 8, 8, 256], P(None, ('grp', 'req'), 'hd'), parts along dimension 1, may hold values from -8 to 8
Outputs:
- merged_cache: bfloat16 [8, 8, 1536, 256], P(('grp', 'req'), 'hd', 'seq'), parts along dimension 0
- attended: bfloat16 [4, 8, 64, 128], P(None, ('grp', 'req'), 'hd'), parts along dimension 1
There are 2 independent parts, one for each index of `grp`. A program takes and returns all parts, laid end to end along the dimension named above; each array names one. Nothing has to cross between parts.
Inputs may be any that keep to these rules, and one draw needn't show every extreme that they name: `targets`: for each request, head and block of 64 evicted rows, at most 32 rows target one block of 384 kept positions; every target is a live position. `kept_counts`: each request has a block with all 384 positions live.
All inputs are finite; a program needn't handle non-finite values.
Results may differ from a plain program's by a relative error of at most 0.0029.
Values may be sent and summed in bfloat16 or wider, within the bound.
No kernel may reach another device: no remote copies, remote signals or barrier semaphores. Data moves between devices by JAX's collectives and lax.ppermute only.
A program may use at most 64 MiB of HBM per device.

v0:
```python
import math

import jax
import jax.numpy as jnp
from jax import lax
from jax.sharding import PartitionSpec as P


def combined_all(part, axis, combine):
    gathered = jax.tree.map(lambda a: lax.all_gather(a, axis), part)

    def take(source):
        return jax.tree.map(lambda a: lax.dynamic_index_in_dim(a, source, 0, False), gathered)

    return lax.fori_loop(
        1, lax.axis_size(axis), lambda source, state: combine(state, take(source)), take(0)
    )


def combine_parts(former, latter):
    former_max, former_sum, former_acc = former
    latter_max, latter_sum, latter_acc = latter
    highest = jnp.maximum(former_max, latter_max)
    former_scale = jnp.exp(former_max - highest)
    latter_scale = jnp.exp(latter_max - highest)
    return (
        highest,
        former_sum * former_scale + latter_sum * latter_scale,
        former_acc * former_scale[..., None] + latter_acc * latter_scale[..., None],
    )


def spread_rows(received, weights, positions, kept_dev):
    columns = jnp.arange(kept_dev, dtype=jnp.int32)
    placing = jnp.where(
        positions[..., None] == columns, weights[..., None], jnp.zeros((), jnp.bfloat16)
    )
    summed = jnp.einsum("rhek,rhec->rhkc", placing, received, preferred_element_type=jnp.float32)
    weight_sum = jnp.sum(placing.astype(jnp.float32), axis=2)
    return (summed, weight_sum)


def partial_block(query_rows, key_rows, value_rows, allowed):
    scale_factor = 1.0 / math.sqrt(query_rows.shape[-1])
    scores = (
        jnp.einsum("rhqd,rhkd->rhqk", query_rows, key_rows, preferred_element_type=jnp.float32)
        * scale_factor
    )
    scores = jnp.where(allowed, scores, -1e30)
    highest = jnp.max(scores, axis=-1)
    exponent = jnp.exp(scores - highest[..., None])
    exponent_sum = jnp.sum(exponent, axis=-1)
    weighted = jnp.einsum(
        "rhqk,rhkd->rhqd",
        exponent.astype(jnp.bfloat16),
        value_rows,
        preferred_element_type=jnp.float32,
    )
    return (highest, exponent_sum, weighted)


def body(cache, evicted, merge_weight, targets, kept_counts, queries, new_rows):
    req_local, head_local, kept_dev, width = cache.shape
    head_dim = width // 2
    shard_count = lax.axis_size("seq")
    evict_dev = evicted.shape[2]
    capacity = max(2, 2 * evict_dev // shard_count)
    holder = targets // kept_dev
    position = targets - holder * kept_dev
    owners = (holder[..., None] == jnp.arange(shard_count, dtype=jnp.int32)).astype(jnp.int32)
    earlier = jnp.cumsum(owners, axis=2) - owners
    ranking = jnp.sum(owners * earlier, axis=-1)
    slot_index = holder * capacity + ranking
    packing = slot_index[..., None] == jnp.arange(shard_count * capacity, dtype=jnp.int32)
    packing_matrix = packing.astype(jnp.bfloat16)
    sent_rows = jnp.einsum(
        "rhes,rhec->rhsc", packing_matrix, evicted, preferred_element_type=jnp.float32
    )
    sent_rows = sent_rows.astype(jnp.bfloat16).reshape(
        req_local, head_local, shard_count, capacity, width
    )
    sent_weight = jnp.einsum(
        "rhes,rhe->rhs", packing_matrix, merge_weight, preferred_element_type=jnp.float32
    )
    sent_weight = sent_weight.astype(jnp.bfloat16).reshape(
        req_local, head_local, shard_count, capacity
    )
    sent_position = jnp.sum(jnp.where(packing, position[..., None], 0), axis=2)
    sent_position = sent_position.reshape(req_local, head_local, shard_count, capacity)
    got_rows, got_weight, got_position = (
        lax.all_to_all(sent_rows, "seq", split_axis=2, concat_axis=2, tiled=True),
        lax.all_to_all(sent_weight, "seq", split_axis=2, concat_axis=2, tiled=True),
        lax.all_to_all(sent_position, "seq", split_axis=2, concat_axis=2, tiled=True),
    )
    slot_total = shard_count * capacity
    summed, weight_sum = spread_rows(
        got_rows.reshape(req_local, head_local, slot_total, width),
        got_weight.reshape(req_local, head_local, slot_total),
        got_position.reshape(req_local, head_local, slot_total),
        kept_dev,
    )
    merged = ((cache.astype(jnp.float32) + summed) / (1.0 + weight_sum)[..., None]).astype(
        jnp.bfloat16
    )
    step_count, _, query_local, _ = queries.shape
    group_size = query_local // head_local
    query_rows = queries.reshape(step_count, req_local, head_local, group_size, head_dim).transpose(
        1, 2, 0, 3, 4
    )
    query_rows = query_rows.reshape(req_local, head_local, step_count * group_size, head_dim)
    living = jnp.arange(kept_dev, dtype=jnp.int32)[None, :] < kept_counts
    cache_max, cache_sum, cache_acc = partial_block(
        query_rows, merged[..., :head_dim], merged[..., head_dim:], living[:, None, None, :]
    )
    shared = combined_all((cache_max, cache_sum, cache_acc), "seq", combine_parts)
    fresh_rows = new_rows.transpose(1, 2, 0, 3)
    step_index = jnp.arange(step_count * group_size, dtype=jnp.int32) // group_size
    allowed = jnp.arange(step_count, dtype=jnp.int32)[None, :] <= step_index[:, None]
    fresh_part = partial_block(
        query_rows, fresh_rows[..., :head_dim], fresh_rows[..., head_dim:], allowed[None, None]
    )
    highest, weight_total, weighted = combine_parts(shared, fresh_part)
    result = (weighted / weight_total[..., None]).astype(jnp.bfloat16)
    attended = result.reshape(req_local, head_local, step_count, group_size, head_dim).transpose(
        2, 0, 1, 3, 4
    )
    attended = attended.reshape(step_count, req_local, query_local, head_dim)
    return (merged, attended)


def solution(mesh):
    return jax.shard_map(
        body,
        mesh=mesh,
        in_specs=(
            P(("grp", "req"), "hd", "seq", None),
            P(("grp", "req"), "hd", "seq", None),
            P(("grp", "req"), "hd", "seq"),
            P(("grp", "req"), "hd", "seq"),
            P(("grp", "req"), "seq"),
            P(None, ("grp", "req"), "hd", None),
            P(None, ("grp", "req"), "hd", None),
        ),
        out_specs=(P(("grp", "req"), "hd", "seq", None), P(None, ("grp", "req"), "hd", None)),
        check_vma=False,
    )
```

profile of v0, /device:TPU:0, one launch (start us, length us, event | category | flops | bytes accessed | tf_op | source)
XLA Modules:
  0.0 84.5 jit_solution(8849968173791281850)
XLA Ops:
  0.6 0.7 multiply_subtract_fusion
  1.8 0.3 select_reduce_fusion.1
  2.1 0.9 %fusion.20 = f32[2,4,1,128]{3,2,1,0:T(1,128)S(1)} fusion(s32[2,4,64]{2,1,0:T(4,128)S(1)} %multiply_add_fusion.1, bf16[2,4,64,1]{2,1,0,3:T(4,128)(2,1)} %bitcast.96), kind=kOutput, calls=%fused_computation.34 | convolution fusion | flops 196608 | bytes 7168 | tf_op jit(solution)/shard_map/rhes,rhe->rhs/dot_general | solution.py:82
  3.2 0.7 reshape.114
  3.8 6.3 %all-to-all-start.1 = ((bf16[4,2,128]{2,1,0:T(2,128)(2,1)}), bf16[4,2,128]{2,1,0:T(2,128)(2,1)S(1)}, u32[]{:S(2)}, u32[]{:S(2)}) async-start(bf16[4,2,128]{2,1,0:T(2,128)(2,1)} %reshape.114), calls=%async_computation.1 | async-start | bytes 4096 | tf_op jit(solution)/shard_map/all_to_all | solution.py:92
  10.2 0.5 convolution_convert_fusion
  11.0 0.7 reshape.112
  11.7 3.9 %all-to-all-done.1 = bf16[4,2,128]{2,1,0:T(2,128)(2,1)S(1)} async-done(((bf16[4,2,128]{2,1,0:T(2,128)(2,1)}), bf16[4,2,128]{2,1,0:T(2,128)(2,1)S(1)}, u32[]{:S(2)}, u32[]{:S(2)}) %all-to-all-start.1) | async-done | bytes 2080 | tf_op jit(solution)/shard_map/all_to_all | solution.py:92
  15.6 3.2 %all-to-all-start = ((s32[4,1,256]{2,1,0:T(1,128)}), s32[4,1,256]{2,1,0:T(1,128)S(1)}, u32[]{:S(2)}, u32[]{:S(2)}) async-start(s32[4,1,256]{2,1,0:T(1,128)} %reshape.112), calls=%async_computation | async-start | bytes 8192 | tf_op jit(solution)/shard_map/all_to_all | solution.py:93
  18.9 0.8 copy.21
  19.7 4.7 %all-to-all-done = s32[4,1,256]{2,1,0:T(1,128)S(1)} async-done(((s32[4,1,256]{2,1,0:T(1,128)}), s32[4,1,256]{2,1,0:T(1,128)S(1)}, u32[]{:S(2)}, u32[]{:S(2)}) %all-to-all-start) | async-done | bytes 4128 | tf_op jit(solution)/shard_map/all_to_all | solution.py:93
  24.4 3.5 %all-to-all-start.2 = ((bf16[2,4,4,32,256]{4,3,1,0,2:T(8,128)(2,1)}), bf16[2,4,4,32,256]{4,3,1,0,2:T(8,128)(2,1)S(1)}, u32[]{:S(2)}, u32[]{:S(2)}) async-start(bf16[2,4,4,32,256]{4,3,1,0,2:T(8,128)(2,1)} %copy.21), calls=%async_computation.2 | async-start | bytes 1048576 | tf_op jit(solution)/shard_map/all_to_all | solution.py:91
  28.4 0.5 broadcast.82
  28.9 0.7 reduce
  29.7 0.5 convert_reduce_fusion
  30.3 9.8 %all-to-all-done.2 = bf16[2,4,4,32,256]{4,3,1,0,2:T(8,128)(2,1)S(1)} async-done(((bf16[2,4,4,32,256]{4,3,1,0,2:T(8,128)(2,1)}), bf16[2,4,4,32,256]{4,3,1,0,2:T(8,128)(2,1)S(1)}, u32[]{:S(2)}, u32[]{:S(2)}) %all-to-all-start.2) | async-done | bytes 524320 | tf_op jit(solution)/shard_map/all_to_all | solution.py:91
  40.1 0.8 divide_convert_fusion
  40.9 0.5 fusion.44
  41.4 13.1 %all-gather = f32[8,4,32]{2,1,0:T(4,128)S(1)} all-gather(f32[2,4,32]{2,1,0:T(4,128)S(1)} %get-tuple-element.206), channel_id=2, replica_groups=mesh['grp'=2,'seq'=4,'req'=2,'hd'=2] {'seq'}, dimensions={0}, use_global_device_ids=true | all-gather | bytes 5120 | tf_op jit(solution)/shard_map/all_gather | solution.py:10
  54.8 0.3 fusion.12
  55.1 13.1 %all-gather.1 = f32[8,4,32]{2,1,0:T(4,128)S(1)} all-gather(f32[2,4,32]{2,1,0:T(4,128)S(1)} %fusion.19), channel_id=3, replica_groups=mesh['grp'=2,'seq'=4,'req'=2,'hd'=2] {'seq'}, dimensions={0}, use_global_device_ids=true | all-gather | bytes 5120 | tf_op jit(solution)/shard_map/all_gather | solution.py:10
  68.2 14.7 %all-gather.2 = f32[8,4,32,128]{3,2,1,0:T(8,128)S(1)} all-gather(f32[2,4,32,128]{3,2,1,0:T(8,128)S(1)} %fusion.12), channel_id=4, replica_groups=mesh['grp'=2,'seq'=4,'req'=2,'hd'=2] {'seq'}, dimensions={0}, use_global_device_ids=true | all-gather | bytes 655360 | tf_op jit(solution)/shard_map/all_gather | solution.py:10
  82.9 0.7 while.19
  83.8 0.6 copy.46
  (47 shorter events, 2.6 us)
Async XLA Ops:
  0.6 9.5 %copy-start = (bf16[2,4,64,256]{3,2,1,0:T(8,128)(2,1)S(1)}, bf16[2,4,64,256]{3,2,1,0:T(8,128)(2,1)}, u32[]{:S(2)}) copy-start(bf16[2,4,64,256]{3,2,1,0:T(8,128)(2,1)} %param.10) | copy-start | bytes 786436
  1.4 18.3 %copy-start.2 = (bf16[4,2,4,256]{3,2,1,0:T(4,128)(2,1)S(1)}, bf16[4,2,4,256]{3,2,1,0:T(4,128)(2,1)}, u32[]{:S(2)}) copy-start(bf16[4,2,4,256]{3,2,1,0:T(4,128)(2,1)} %param.15) | copy-start | bytes 49156
  3.1 24.8 %copy-start.5 = (bf16[4,2,32,128]{3,2,1,0:T(8,128)(2,1)S(1)}, bf16[4,2,32,128]{3,2,1,0:T(8,128)(2,1)}, u32[]{:S(2)}) copy-start(bf16[4,2,32,128]{3,2,1,0:T(8,128)(2,1)} %param.14) | copy-start | bytes 196612
  3.8 11.8 %all-to-all-start.1 = ((bf16[4,2,128]{2,1,0:T(2,128)(2,1)}), bf16[4,2,128]{2,1,0:T(2,128)(2,1)S(1)}, u32[]{:S(2)}, u32[]{:S(2)}) async-start(bf16[4,2,128]{2,1,0:T(2,128)(2,1)} %reshape.114), calls=%async_computation.1 | async-start | bytes 4096 | tf_op jit(solution)/shard_map/all_to_all | solution.py:92
  10.2 18.0 %copy-start.3 = (s32[2,1]{0,1:T(1,128)S(1)}, s32[2,1]{0,1:T(1,128)}, u32[]{:S(2)}) copy-start(s32[2,1]{0,1:T(1,128)} %param.13) | copy-start | bytes 28
  15.6 8.8 %all-to-all-start = ((s32[4,1,256]{2,1,0:T(1,128)}), s32[4,1,256]{2,1,0:T(1,128)S(1)}, u32[]{:S(2)}, u32[]{:S(2)}) async-start(s32[4,1,256]{2,1,0:T(1,128)} %reshape.112), calls=%async_computation | async-start | bytes 8192 | tf_op jit(solution)/shard_map/all_to_all | solution.py:93
  18.9 21.2 %copy-start.4 = (bf16[2,4,384,256]{3,2,1,0:T(8,128)(2,1)S(1)}, bf16[2,4,384,256]{3,2,1,0:T(8,128)(2,1)}, u32[]{:S(2)}) copy-start(bf16[2,4,384,256]{3,2,1,0:T(8,128)(2,1)} %param.9) | copy-start | bytes 4718596
  24.4 15.6 %all-to-all-start.2 = ((bf16[2,4,4,32,256]{4,3,1,0,2:T(8,128)(2,1)}), bf16[2,4,4,32,256]{4,3,1,0,2:T(8,128)(2,1)S(1)}, u32[]{:S(2)}, u32[]{:S(2)}) async-start(bf16[2,4,4,32,256]{4,3,1,0,2:T(8,128)(2,1)} %copy.21), calls=%async_computation.2 | async-start | bytes 1048576 | tf_op jit(solution)/shard_map/all_to_all | solution.py:91
  40.9 14.2 %copy-start.1 = (bf16[2,4,384,256]{3,2,1,0:T(8,128)(2,1)}, bf16[2,4,384,256]{3,2,1,0:T(8,128)(2,1)S(1)}, u32[]{:S(2)}) copy-start(bf16[2,4,384,256]{3,2,1,0:T(8,128)(2,1)S(1)} %divide_convert_fusion) | copy-start | bytes 4718596
where the time goes:
time: 84.8 us; the launch traced here: 84.5 us
  blocking collectives  40.9 us (48%)
  waiting for transfers between devices  18.4 us (22%)
  starting transfers between devices  13 us (15%)
  local copies, waits for them, and re-layouts  3.97 us (5%)
  other arithmetic  3.78 us (4%)
  matrix products  3.46 us (4%)
    all_gather x3, blocking collectives, combined_all(): gathered = jax.tree.map(lambda a: lax.all_gather(a, axis), part)  40.9 us
    all_to_all x1, waiting for transfers between devices, body(): lax.all_to_all(sent_rows, 'seq', split_axis=2, concat_axis=2, tiled=True)  9.8 us
    all_to_all x1, starting transfers between devices, body(): lax.all_to_all(sent_weight, 'seq', split_axis=2, concat_axis=2, tiled=True)  6.32 us
    all_to_all x1, waiting for transfers between devices, body(): lax.all_to_all(sent_position, 'seq', split_axis=2, concat_axis=2, tiled=T...  4.67 us
    all_to_all x1, waiting for transfers between devices, body(): lax.all_to_all(sent_weight, 'seq', split_axis=2, concat_axis=2, tiled=True)  3.94 us
    all_to_all x1, starting transfers between devices, body(): lax.all_to_all(sent_rows, 'seq', split_axis=2, concat_axis=2, tiled=True)  3.47 us
    all_to_all x1, starting transfers between devices, body(): lax.all_to_all(sent_position, 'seq', split_axis=2, concat_axis=2, tiled=T...  3.25 us
  transfers between devices with their start and end apart: 3, of which 3 were waited for; matrix products, arithmetic and copies ran while one was open for 6% of the time, Pallas kernels for 0%

commit v1 on v0

v1 whole, which is shorter than its diff:
```python
import functools
import math

import jax
import jax.numpy as jnp
from jax import lax
from jax.experimental import pallas as pl
from jax.experimental.pallas import tpu as pltpu
from jax.sharding import PartitionSpec as P

META_ROWS = 16
STAT_ROWS = 8
VMEM_BYTES = 32 * 1024 * 1024


def dot(a, b, contract):
    return lax.dot_general(a, b, (contract, ((), ())), preferred_element_type=jnp.float32)


def pack_kernel(shards, capacity, kept_dev, evicted_ref, weight_ref, target_ref, *message_refs):
    pairs, evict_dev, width = evicted_ref.shape
    slots = shards * capacity
    me = lax.axis_index("seq")
    targets = target_ref[...]
    holder = jnp.zeros_like(targets)
    for block in range(1, shards):
        holder += (targets >= block * kept_dev).astype(jnp.int32)
    centred = targets - holder * kept_dev - kept_dev // 2
    distance = jnp.where(holder >= me, holder - me, holder - me + shards)
    owned = jnp.concatenate(
        [(distance == k).astype(jnp.float32) for k in range(shards)], axis=0
    )
    before = lax.broadcasted_iota(jnp.int32, (evict_dev, evict_dev), 0) < lax.broadcasted_iota(
        jnp.int32, (evict_dev, evict_dev), 1
    )
    prefix = dot(owned.astype(jnp.bfloat16), before.astype(jnp.bfloat16), ((1,), (0,)))
    ranked = owned * prefix
    rank = ranked[0:pairs]
    for k in range(1, shards):
        rank += ranked[k * pairs : (k + 1) * pairs]
    slot = distance * capacity + rank.astype(jnp.int32)
    facts = jnp.concatenate(
        [weight_ref[...].astype(jnp.float32), centred.astype(jnp.float32)], axis=0
    ).astype(jnp.bfloat16)
    slot_index = lax.broadcasted_iota(jnp.int32, (slots, evict_dev), 0)
    pair_index = lax.broadcasted_iota(jnp.int32, (pairs, slots), 0)
    weights = jnp.zeros((pairs, slots), jnp.float32)
    positions = jnp.zeros((pairs, slots), jnp.float32)
    rows = []
    for p in range(pairs):
        placing = (slot_index == slot[p : p + 1, :]).astype(jnp.float32).astype(jnp.bfloat16)
        rows.append(dot(placing, evicted_ref[p], ((1,), (0,))))
        placed = dot(facts, placing, ((1,), (1,)))
        weights = jnp.where(pair_index == p, placed[0:pairs], weights)
        positions = jnp.where(pair_index == p, placed[pairs : 2 * pairs], positions)
    meta = jnp.concatenate([weights, positions], axis=1)
    meta = jnp.concatenate([meta, jnp.zeros((META_ROWS - pairs, 2 * slots), jnp.float32)], axis=0)
    meta = meta.astype(jnp.bfloat16)
    for k in range(shards):
        message = [r[k * capacity : (k + 1) * capacity] for r in rows]
        message_refs[k][0 : pairs * capacity, :] = jnp.concatenate(message, axis=0).astype(
            jnp.bfloat16
        )
        message_refs[k][pairs * capacity : pairs * capacity + META_ROWS, :] = meta


def merge_kernel(shards, capacity, heads, *refs):
    cache_ref, query_ref, count_ref = refs[:3]
    message_refs = refs[3 : 3 + shards]
    merged_ref, partial_ref, cache_buf, merged_buf, in_sem, out_sem = refs[3 + shards :]
    pairs, kept_dev, width = cache_buf.shape
    head_dim = width // 2
    rows_each = query_ref.shape[1]
    slots = shards * capacity
    scale = 1.0 / math.sqrt(head_dim)
    loads = [
        pltpu.make_async_copy(cache_ref.at[p], cache_buf.at[p], in_sem.at[p]) for p in range(pairs)
    ]
    stores = [
        pltpu.make_async_copy(merged_buf.at[p], merged_ref.at[p], out_sem.at[p])
        for p in range(pairs)
    ]
    for load in loads:
        load.start()
    lane = lax.broadcasted_iota(jnp.int32, (pairs, slots), 1)
    weights = jnp.zeros((pairs, slots), jnp.float32)
    positions = jnp.zeros((pairs, slots), jnp.float32)
    received = []
    for k in range(shards):
        meta = message_refs[k][pairs * capacity : pairs * capacity + META_ROWS, :]
        meta = meta.astype(jnp.float32)[0:pairs]
        mine = jnp.logical_and(lane >= k * capacity, lane < (k + 1) * capacity)
        weights = jnp.where(mine, meta[:, 0:slots], weights)
        positions = jnp.where(mine, meta[:, slots : 2 * slots], positions)
        if capacity % 16:
            received.append(message_refs[k][0 : pairs * capacity, :].astype(jnp.float32))
    positions = (positions + float(kept_dev // 2)).astype(jnp.int32)
    kept_index = lax.broadcasted_iota(jnp.int32, (kept_dev, slots), 0)
    column = lax.broadcasted_iota(jnp.int32, (rows_each, kept_dev), 1)
    ones = jnp.ones((slots, head_dim), jnp.bfloat16)
    tops, totals = [], []
    for p in range(pairs):
        if capacity % 16:
            rows = [r[p * capacity : (p + 1) * capacity] for r in received]
            rows = jnp.concatenate(rows, axis=0).astype(jnp.bfloat16)
        else:
            rows = [m[p * capacity : (p + 1) * capacity, :] for m in message_refs]
            rows = jnp.concatenate(rows, axis=0)
        placing = jnp.where(kept_index == positions[p : p + 1, :], weights[p : p + 1, :], 0.0)
        placing = placing.astype(jnp.bfloat16)
        summed = dot(placing, rows, ((1,), (0,)))
        share = 1.0 / (1.0 + dot(placing, ones, ((1,), (0,))))
        loads[p].wait()
        stored = cache_buf[p].astype(jnp.float32) + summed
        keys = (stored[:, 0:head_dim] * share).astype(jnp.bfloat16)
        values = (stored[:, head_dim:] * share).astype(jnp.bfloat16)
        merged_buf[p, :, 0:head_dim] = keys
        merged_buf[p, :, head_dim:] = values
        stores[p].start()
        scores = dot(query_ref[p], keys, ((1,), (1,))) * scale
        scores = jnp.where(column < count_ref[p // heads, 0], scores, -1e30)
        top = jnp.max(scores, axis=1, keepdims=True)
        exponent = jnp.exp(scores - top)
        tops.append(top)
        totals.append(jnp.sum(exponent, axis=1, keepdims=True))
        partial_ref[p * rows_each : (p + 1) * rows_each, :] = dot(
            exponent.astype(jnp.bfloat16), values, ((1,), (0,))
        )
    stat_lane = lax.broadcasted_iota(jnp.int32, (heads * rows_each, head_dim), 1)
    stats = []
    for first in range(0, pairs, heads):
        top = jnp.concatenate(tops[first : first + heads], axis=0)
        total = jnp.concatenate(totals[first : first + heads], axis=0)
        both = jnp.where(stat_lane == 0, top, jnp.where(stat_lane == 1, total, 0.0))
        stats.append(jnp.transpose(both)[0:2, :])
    stats.append(jnp.zeros((STAT_ROWS - 2 * (pairs // heads), head_dim), jnp.float32))
    partial_ref[pairs * rows_each : pairs * rows_each + STAT_ROWS, :] = jnp.concatenate(
        stats, axis=0
    )
    for store in stores:
        store.wait()


def combine_kernel(shards, heads, *refs):
    partial_refs = refs[:shards]
    fresh_top_ref, fresh_total_ref, fresh_ref, out_ref, ordered = refs[shards:]
    steps, requests, query_local, head_dim = out_ref.shape
    group = query_local // heads
    rows_each = steps * group
    rows_request = heads * rows_each
    me = lax.axis_index("seq")
    for k in range(shards):
        source = jnp.where(me >= k, me - k, me - k + shards)
        ordered[source] = partial_refs[k][...]
    for r in range(requests):
        tops, totals = [fresh_top_ref[r : r + 1, :]], [fresh_total_ref[r : r + 1, :]]
        for b in range(shards):
            first = requests * rows_request + 2 * r
            tops.append(ordered[b, first : first + 1, :])
            totals.append(ordered[b, first + 1 : first + 2, :])
        highest = functools.reduce(jnp.maximum, tops)
        scales = [jnp.exp(top - highest) for top in tops]
        total = sum(a * b for a, b in zip(totals, scales))
        factors = jnp.concatenate([s / total for s in scales], axis=0)
        padding = -(shards + 1) % 8
        if padding:
            factors = jnp.concatenate(
                [factors, jnp.zeros((padding, rows_request), jnp.float32)], axis=0
            )
        factors = jnp.transpose(factors)
        first = r * rows_request
        result = fresh_ref[first : first + rows_request, :] * factors[:, 0:1]
        for b in range(shards):
            result += ordered[b, first : first + rows_request, :] * factors[:, b + 1 : b + 2]
        for s in range(steps):
            pieces = [
                result[h * rows_each + s * group : h * rows_each + (s + 1) * group]
                for h in range(heads)
            ]
            out_ref[s, r] = jnp.concatenate(pieces, axis=0).astype(jnp.bfloat16)


def fresh_block(query_rows, fresh_rows, group):
    head_dim = query_rows.shape[-1]
    scores = jnp.einsum(
        "pqd,pjd->pqj", query_rows, fresh_rows[..., :head_dim], preferred_element_type=jnp.float32
    ) * (1.0 / math.sqrt(head_dim))
    step_index = jnp.arange(query_rows.shape[1], dtype=jnp.int32) // group
    allowed = jnp.arange(fresh_rows.shape[1], dtype=jnp.int32)[None, :] <= step_index[:, None]
    scores = jnp.where(allowed[None], scores, -1e30)
    top = jnp.max(scores, axis=-1)
    exponent = jnp.exp(scores - top[..., None])
    weighted = jnp.einsum(
        "pqj,pjd->pqd",
        exponent.astype(jnp.bfloat16),
        fresh_rows[..., head_dim:],
        preferred_element_type=jnp.float32,
    )
    return (top, jnp.sum(exponent, axis=-1), weighted)


def body(cache, evicted, merge_weight, targets, kept_counts, queries, new_rows):
    req_local, head_local, kept_dev, width = cache.shape
    head_dim = width // 2
    shards = lax.axis_size("seq")
    evict_dev = evicted.shape[2]
    capacity = max(2, 2 * evict_dev // shards)
    pairs = req_local * head_local
    steps, _, query_local, _ = queries.shape
    group = query_local // head_local
    rows_each = steps * group
    vmem = pl.BlockSpec(memory_space=pltpu.VMEM)
    smem = pl.BlockSpec(memory_space=pltpu.SMEM)
    anywhere = pl.BlockSpec(memory_space=pl.ANY)
    params = pltpu.CompilerParams(vmem_limit_bytes=VMEM_BYTES)

    message = jax.ShapeDtypeStruct((pairs * capacity + META_ROWS, width), jnp.bfloat16)
    messages = pl.pallas_call(
        functools.partial(pack_kernel, shards, capacity, kept_dev),
        out_shape=[message] * shards,
        in_specs=[vmem] * 3,
        out_specs=[vmem] * shards,
        compiler_params=params,
        name="pack",
    )(
        evicted.reshape(pairs, evict_dev, width),
        merge_weight.reshape(pairs, evict_dev),
        targets.reshape(pairs, evict_dev),
    )

    def shifted(array, k):
        return lax.ppermute(array, "seq", [(i, (i + k) % shards) for i in range(shards)])

    messages = [messages[0]] + [shifted(messages[k], k) for k in range(1, shards)]

    query_rows = queries.reshape(steps, req_local, head_local, group, head_dim)
    query_rows = query_rows.transpose(1, 2, 0, 3, 4).reshape(pairs, rows_each, head_dim)
    fresh_rows = new_rows.transpose(1, 2, 0, 3).reshape(pairs, steps, width)
    fresh_top, fresh_total, fresh = fresh_block(query_rows, fresh_rows, group)

    merged, partial = pl.pallas_call(
        functools.partial(merge_kernel, shards, capacity, head_local),
        out_shape=[
            jax.ShapeDtypeStruct((pairs, kept_dev, width), jnp.bfloat16),
            jax.ShapeDtypeStruct((pairs * rows_each + STAT_ROWS, head_dim), jnp.float32),
        ],
        in_specs=[anywhere, vmem, smem] + [vmem] * shards,
        out_specs=[anywhere, vmem],
        scratch_shapes=[
            pltpu.VMEM((pairs, kept_dev, width), jnp.bfloat16),
            pltpu.VMEM((pairs, kept_dev, width), jnp.bfloat16),
            pltpu.SemaphoreType.DMA((pairs,)),
            pltpu.SemaphoreType.DMA((pairs,)),
        ],
        compiler_params=params,
        name="merge",
    )(cache.reshape(pairs, kept_dev, width), query_rows, kept_counts, *messages)

    partials = [partial] + [shifted(partial, k) for k in range(shards - 1, 0, -1)][::-1]

    attended = pl.pallas_call(
        functools.partial(combine_kernel, shards, head_local),
        out_shape=jax.ShapeDtypeStruct(queries.shape, jnp.bfloat16),
        in_specs=[vmem] * (shards + 3),
        out_specs=vmem,
        scratch_shapes=[pltpu.VMEM((shards,) + partial.shape, jnp.float32)],
        compiler_params=params,
        name="combine",
    )(
        *partials,
        fresh_top.reshape(req_local, head_local * rows_each),
        fresh_total.reshape(req_local, head_local * rows_each),
        fresh.reshape(pairs * rows_each, head_dim),
    )
    return (merged.reshape(cache.shape), attended)


def solution(mesh):
    return jax.shard_map(
        body,
        mesh=mesh,
        in_specs=(
            P(("grp", "req"), "hd", "seq", None),
            P(("grp", "req"), "hd", "seq", None),
            P(("grp", "req"), "hd", "seq"),
            P(("grp", "req"), "hd", "seq"),
            P(("grp", "req"), "seq"),
            P(None, ("grp", "req"), "hd", None),
            P(None, ("grp", "req"), "hd", None),
        ),
        out_specs=(P(("grp", "req"), "hd", "seq", None), P(None, ("grp", "req"), "hd", None)),
        check_vma=False,
    )
```

time: 84.8 us -> 42.7 us (0.50)
  the two profiles are of different devices: /device:TPU:0 before, /device:TPU:13 now
where the time goes in v1:
time: 42.7 us; the launch traced here: 42.4 us
  waiting for transfers between devices  20.3 us (48%)
  Pallas kernels  9.18 us (21%)
  local copies, waits for them, and re-layouts  6.19 us (14%)
  starting transfers between devices  5.63 us (13%)
  between operations  0.69 us (2%)
    ppermute x6, waiting for transfers between devices, shifted(): lax.ppermute(array, 'seq', [(i, (i + k) % shards) for i in range(shards)])  20.3 us
    pallas_call x1, Pallas kernels, body(): pl.pallas_call(functools.partial(merge_kernel, shards, capacity, head_loc...  7.49 us
    ppermute x6, starting transfers between devices, shifted(): lax.ppermute(array, 'seq', [(i, (i + k) % shards) for i in range(shards)])  5.63 us
    unnamed x9, local copies, waits for them, and re-layouts  4.46 us
    pallas_call x1, Pallas kernels, body(): pl.pallas_call(functools.partial(combine_kernel, shards, head_local), out...  1.16 us
  transfers between devices with their start and end apart: 6, of which 5 were waited for; matrix products, arithmetic and copies ran while one was open for 7% of the time, Pallas kernels for 0%

profile of v1, /device:TPU:13, one launch (start us, length us, event | category | flops | bytes accessed | tf_op | source)
XLA Modules:
  0.0 42.4 jit_solution(13030630629206397348)
XLA Ops:
  0.6 0.9 %copy-done.1 = bf16[2,4,64,256]{3,2,1,0:T(8,128)(2,1)S(1)} copy-done((bf16[2,4,64,256]{3,2,1,0:T(8,128)(2,1)S(1)}, bf16[2,4,64,256]{3,2,1,0:T(8,128)(2,1)}, u32[]{:S(2)}) %copy-start.1) | copy-done | bytes 262168
  1.6 0.7 %copy-done.2 = s32[2,4,64]{2,1,0:T(4,128)S(1)} copy-done((s32[2,4,64]{2,1,0:T(4,128)S(1)}, s32[2,4,64]{2,1,0:T(4,128)}, u32[]{:S(2)}) %copy-start.2) | copy-done | bytes 2072
  2.3 0.7 %copy-done.3 = bf16[2,4,64]{2,1,0:T(4,128)(2,1)S(1)} copy-done((bf16[2,4,64]{2,1,0:T(4,128)(2,1)S(1)}, bf16[2,4,64]{2,1,0:T(4,128)(2,1)}, u32[]{:S(2)}) %copy-start.3) | copy-done | bytes 1048
  3.0 0.5 %pack.1 = (bf16[272,256]{1,0:T(8,128)(2,1)S(1)}, bf16[272,256]{1,0:T(8,128)(2,1)S(1)}, bf16[272,256]{1,0:T(8,128)(2,1)S(1)}, bf16[272,256]{1,0:T(8,128)(2,1)S(1)}) custom-call(bf16[8,64,256]{2,1,0:T(8,128)(2,1)S(1)} %bitcast.17, bf16[8,64]{1,0:T(8,128)(2,1)S(1)} %bitcast.19, s32[8,64]{1,0:T(8,128)S(1)} %bitcast.18), custom_call_target="tpu_custom_call" | custom-call | tf_op jit(solution)/shard_map/pack/pallas_call | solution.py:218
  3.5 1.3 %collective-permute-start = (bf16[272,256]{1,0:T(8,128)(2,1)S(1)}, bf16[272,256]{1,0:T(8,128)(2,1)S(1)}, u32[]{:S(2)}, u32[]{:S(2)}) collective-permute-start(bf16[272,256]{1,0:T(8,128)(2,1)S(1)} %get-tuple-element.9), channel_id=1, source_target_pairs={{0,4},{4,8},{8,12},{12,0},{1,5},{5,9},{9,13},{13,1},{2,6},{6,10},{... | collective-permute-start | bytes 417800 | tf_op jit(solution)/shard_map/ppermute | solution.py:232
  4.8 1.1 %collective-permute-start.1 = (bf16[272,256]{1,0:T(8,128)(2,1)S(1)}, bf16[272,256]{1,0:T(8,128)(2,1)S(1)}, u32[]{:S(2)}, u32[]{:S(2)}) collective-permute-start(bf16[272,256]{1,0:T(8,128)(2,1)S(1)} %get-tuple-element.10), channel_id=1, source_target_pairs={{0,8},{4,12},{8,0},{12,4},{1,9},{5,13},{9,1},{13,5},{2,10},{6,14},... | collective-permute-start | bytes 417800 | tf_op jit(solution)/shard_map/ppermute | solution.py:232
  5.9 1.4 %collective-permute-start.2 = (bf16[272,256]{1,0:T(8,128)(2,1)S(1)}, bf16[272,256]{1,0:T(8,128)(2,1)S(1)}, u32[]{:S(2)}, u32[]{:S(2)}) collective-permute-start(bf16[272,256]{1,0:T(8,128)(2,1)S(1)} %get-tuple-element.11), channel_id=1, source_target_pairs={{0,12},{4,0},{8,4},{12,8},{1,13},{5,1},{9,5},{13,9},{2,14},{6,2},{... | collective-permute-start | bytes 417800 | tf_op jit(solution)/shard_map/ppermute | solution.py:232
  7.3 0.9 %copy.9 = bf16[4,2,4,8,128]{4,3,0,2,1:T(8,128)(2,1)S(1)} copy(bf16[4,2,4,8,128]{4,3,2,1,0:T(8,128)(2,1)} %bitcast.20) | data formatting | bytes 131072 | tf_op jit(solution)/shard_map/reshape | solution.py:236
  8.2 0.7 %copy.11 = bf16[2,4,4,256]{3,2,1,0:T(4,128)(2,1)S(1)} copy(bf16[2,4,4,256]{3,1,0,2:T(4,128)(2,1)} %bitcast.23) | data formatting | bytes 32768 | tf_op jit(solution)/shard_map/transpose | solution.py:238
  8.9 0.2 fusion.8
  9.1 0.7 %copy.10.refs_2_ = s32[2,1]{1,0:T(2,128)S(1)} copy(s32[2,1]{0,1:T(1,128)} %param.11) | data formatting | bytes 16 | tf_op args[4]
  9.8 0.1 reshape.78.refs_4_
  9.9 0.1 reshape.79.refs_5_
  10.0 6.1 %collective-permute-done.1.refs_5_ = bf16[272,256]{1,0:T(8,128)(2,1)S(1)} collective-permute-done((bf16[272,256]{1,0:T(8,128)(2,1)S(1)}, bf16[272,256]{1,0:T(8,128)(2,1)S(1)}, u32[]{:S(2)}, u32[]{:S(2)}) %collective-permute-start.1) | collective-permute-done | bytes 139296 | tf_op jit(solution)/shard_map/ppermute | solution.py:232
  16.1 2.8 %collective-permute-done.2.refs_6_ = bf16[272,256]{1,0:T(8,128)(2,1)S(1)} collective-permute-done((bf16[272,256]{1,0:T(8,128)(2,1)S(1)}, bf16[272,256]{1,0:T(8,128)(2,1)S(1)}, u32[]{:S(2)}, u32[]{:S(2)}) %collective-permute-start.2) | collective-permute-done | bytes 139296 | tf_op jit(solution)/shard_map/ppermute | solution.py:232
  18.9 1.4 %copy-done = bf16[2,4,384,256]{3,2,1,0:T(8,128)(2,1)S(1)} copy-done((bf16[2,4,384,256]{3,2,1,0:T(8,128)(2,1)S(1)}, bf16[2,4,384,256]{3,2,1,0:T(8,128)(2,1)}, u32[]{:S(2)}) %copy-start) | copy-done | bytes 1572888
  20.3 7.5 %merge.1 = (bf16[8,384,256]{2,1,0:T(8,128)(2,1)}, f32[264,128]{1,0:T(8,128)S(1)}) custom-call(bf16[8,384,256]{2,1,0:T(8,128)(2,1)S(1)} %bitcast.13, bf16[8,32,128]{2,1,0:T(8,128)(2,1)S(1)} %bitcast.16, s32[2,1]{1,0:T(2,128)S(1)} %copy.10.refs_2_, bf16[272,256]{1,0:T(8,128)(2,1)S(1)} %get-tuple-element.8.refs_3_, ...), custom_call_target="tpu_custom_call" | custom-call | tf_op jit(solution)/shard_map/merge/pallas_call | solution.py:241
  27.9 0.4 collective-permute-start.4
  28.3 1.4 %collective-permute-start.5 = (f32[264,128]{1,0:T(8,128)S(1)}, f32[264,128]{1,0:T(8,128)S(1)}, u32[]{:S(2)}, u32[]{:S(2)}) collective-permute-start(f32[264,128]{1,0:T(8,128)S(1)} %get-tuple-element.13.refs_0_), channel_id=1, source_target_pairs={{0,12},{4,0},{8,4},{12,8},{1,13},{5,1},{9,5},{13,9},{2,14},{6,2},{... | collective-permute-start | bytes 405512 | tf_op jit(solution)/shard_map/ppermute | solution.py:232
  29.6 0.2 fusion.3
  29.9 2.7 %collective-permute-done.3.refs_1_ = f32[264,128]{1,0:T(8,128)S(1)} collective-permute-done((f32[264,128]{1,0:T(8,128)S(1)}, f32[264,128]{1,0:T(8,128)S(1)}, u32[]{:S(2)}, u32[]{:S(2)}) %collective-permute-start.3) | collective-permute-done | bytes 135200 | tf_op jit(solution)/shard_map/ppermute | solution.py:232
  32.6 6.8 %collective-permute-done.4.refs_2_ = f32[264,128]{1,0:T(8,128)S(1)} collective-permute-done((f32[264,128]{1,0:T(8,128)S(1)}, f32[264,128]{1,0:T(8,128)S(1)}, u32[]{:S(2)}, u32[]{:S(2)}) %collective-permute-start.4) | collective-permute-done | bytes 135200 | tf_op jit(solution)/shard_map/ppermute | solution.py:232
  39.4 1.8 %collective-permute-done.5.refs_3_ = f32[264,128]{1,0:T(8,128)S(1)} collective-permute-done((f32[264,128]{1,0:T(8,128)S(1)}, f32[264,128]{1,0:T(8,128)S(1)}, u32[]{:S(2)}, u32[]{:S(2)}) %collective-permute-start.5) | collective-permute-done | bytes 135200 | tf_op jit(solution)/shard_map/ppermute | solution.py:232
  41.2 1.2 %combine.1 = bf16[4,2,32,128]{3,2,1,0:T(8,128)(2,1)} custom-call(f32[264,128]{1,0:T(8,128)S(1)} %get-tuple-element.13.refs_0_, f32[264,128]{1,0:T(8,128)S(1)} %collective-permute-done.3.refs_1_, f32[264,128]{1,0:T(8,128)S(1)} %collective-permute-done.4.refs_2_, f32[264,128]{1,0:T(8,128)S(1)} %collective-permute-done.5.refs_3_, ...), custom_call_target="tpu_custom_call" | custom-call | tf_op jit(solution)/shard_map/combine/pallas_call | solution.py:261
  (9 shorter events, 0.1 us)
Async XLA Ops:
  0.6 1.0 %copy-start.1 = (bf16[2,4,64,256]{3,2,1,0:T(8,128)(2,1)S(1)}, bf16[2,4,64,256]{3,2,1,0:T(8,128)(2,1)}, u32[]{:S(2)}) copy-start(bf16[2,4,64,256]{3,2,1,0:T(8,128)(2,1)} %param.8) | copy-start | bytes 786436
  1.6 0.7 %copy-start.2 = (s32[2,4,64]{2,1,0:T(4,128)S(1)}, s32[2,4,64]{2,1,0:T(4,128)}, u32[]{:S(2)}) copy-start(s32[2,4,64]{2,1,0:T(4,128)} %param.10) | copy-start | bytes 6148
  2.3 0.7 %copy-start.3 = (bf16[2,4,64]{2,1,0:T(4,128)(2,1)S(1)}, bf16[2,4,64]{2,1,0:T(4,128)(2,1)}, u32[]{:S(2)}) copy-start(bf16[2,4,64]{2,1,0:T(4,128)(2,1)} %param.9) | copy-start | bytes 3076
  3.5 6.5 %collective-permute-start = (bf16[272,256]{1,0:T(8,128)(2,1)S(1)}, bf16[272,256]{1,0:T(8,128)(2,1)S(1)}, u32[]{:S(2)}, u32[]{:S(2)}) collective-permute-start(bf16[272,256]{1,0:T(8,128)(2,1)S(1)} %get-tuple-element.9), channel_id=1, source_target_pairs={{0,4},{4,8},{8,12},{12,0},{1,5},{5,9},{9,13},{13,1},{2,6},{6,10},{... | collective-permute-start | bytes 417800 | tf_op jit(solution)/shard_map/ppermute | solution.py:232
  4.8 11.3 %collective-permute-start.1 = (bf16[272,256]{1,0:T(8,128)(2,1)S(1)}, bf16[272,256]{1,0:T(8,128)(2,1)S(1)}, u32[]{:S(2)}, u32[]{:S(2)}) collective-permute-start(bf16[272,256]{1,0:T(8,128)(2,1)S(1)} %get-tuple-element.10), channel_id=1, source_target_pairs={{0,8},{4,12},{8,0},{12,4},{1,9},{5,13},{9,1},{13,5},{2,10},{6,14},... | collective-permute-start | bytes 417800 | tf_op jit(solution)/shard_map/ppermute | solution.py:232
  5.9 13.0 %collective-permute-start.2 = (bf16[272,256]{1,0:T(8,128)(2,1)S(1)}, bf16[272,256]{1,0:T(8,128)(2,1)S(1)}, u32[]{:S(2)}, u32[]{:S(2)}) collective-permute-start(bf16[272,256]{1,0:T(8,128)(2,1)S(1)} %get-tuple-element.11), channel_id=1, source_target_pairs={{0,12},{4,0},{8,4},{12,8},{1,13},{5,1},{9,5},{13,9},{2,14},{6,2},{... | collective-permute-start | bytes 417800 | tf_op jit(solution)/shard_map/ppermute | solution.py:232
  18.9 1.4 %copy-start = (bf16[2,4,384,256]{3,2,1,0:T(8,128)(2,1)S(1)}, bf16[2,4,384,256]{3,2,1,0:T(8,128)(2,1)}, u32[]{:S(2)}) copy-start(bf16[2,4,384,256]{3,2,1,0:T(8,128)(2,1)} %param.7) | copy-start | bytes 4718596
  27.8 4.7 %collective-permute-start.3 = (f32[264,128]{1,0:T(8,128)S(1)}, f32[264,128]{1,0:T(8,128)S(1)}, u32[]{:S(2)}, u32[]{:S(2)}) collective-permute-start(f32[264,128]{1,0:T(8,128)S(1)} %get-tuple-element.13.refs_0_), channel_id=1, source_target_pairs={{0,4},{4,8},{8,12},{12,0},{1,5},{5,9},{9,13},{13,1},{2,6},{6,10},{... | collective-permute-start | bytes 405512 | tf_op jit(solution)/shard_map/ppermute | solution.py:232
  27.9 11.5 %collective-permute-start.4 = (f32[264,128]{1,0:T(8,128)S(1)}, f32[264,128]{1,0:T(8,128)S(1)}, u32[]{:S(2)}, u32[]{:S(2)}) collective-permute-start(f32[264,128]{1,0:T(8,128)S(1)} %get-tuple-element.13.refs_0_), channel_id=1, source_target_pairs={{0,8},{4,12},{8,0},{12,4},{1,9},{5,13},{9,1},{13,5},{2,10},{6,14},... | collective-permute-start | bytes 405512 | tf_op jit(solution)/shard_map/ppermute | solution.py:232
  28.3 12.9 %collective-permute-start.5 = (f32[264,128]{1,0:T(8,128)S(1)}, f32[264,128]{1,0:T(8,128)S(1)}, u32[]{:S(2)}, u32[]{:S(2)}) collective-permute-start(f32[264,128]{1,0:T(8,128)S(1)} %get-tuple-element.13.refs_0_), channel_id=1, source_target_pairs={{0,12},{4,0},{8,4},{12,8},{1,13},{5,1},{9,5},{13,9},{2,14},{6,2},{... | collective-permute-start | bytes 405512 | tf_op jit(solution)/shard_map/ppermute | solution.py:232

commit v2 on v1

--- a/solution.py
+++ b/solution.py
@@ -9,18 +9,31 @@
 from jax.sharding import PartitionSpec as P
 
 META_ROWS = 16
-STAT_ROWS = 8
-VMEM_BYTES = 32 * 1024 * 1024
+STATS = 4
+CODE_MAX = 32767.0
+LEVELS = 16.0
+SMALLEST = 1e-36
+FRACTION = 2.0**30
+VMEM_BYTES = 8 * 1024 * 1024
 
 
 def dot(a, b, contract):
     return lax.dot_general(a, b, (contract, ((), ())), preferred_element_type=jnp.float32)
 
 
-def pack_kernel(shards, capacity, kept_dev, evicted_ref, weight_ref, target_ref, *message_refs):
+def pack_kernel(shards, capacity, kept_dev, *refs):
+    message_refs = refs[3 : 3 + shards]
+    evicted_ref, weight_ref, target_ref, sems = refs[3 + shards :]
+    loads = [
+        pltpu.make_async_copy(refs[i], refs[3 + shards + i], sems.at[i]) for i in (2, 1, 0)
+    ]
+    for load in loads:
+        load.start()
     pairs, evict_dev, width = evicted_ref.shape
     slots = shards * capacity
     me = lax.axis_index("seq")
+    loads[0].wait()
+    loads[1].wait()
     targets = target_ref[...]
     holder = jnp.zeros_like(targets)
     for block in range(1, shards):
@@ -47,6 +60,7 @@
     weights = jnp.zeros((pairs, slots), jnp.float32)
     positions = jnp.zeros((pairs, slots), jnp.float32)
     rows = []
+    loads[2].wait()
     for p in range(pairs):
         placing = (slot_index == slot[p : p + 1, :]).astype(jnp.float32).astype(jnp.bfloat16)
         rows.append(dot(placing, evicted_ref[p], ((1,), (0,))))
@@ -64,24 +78,21 @@
         message_refs[k][pairs * capacity : pairs * capacity + META_ROWS, :] = meta
 
 
+def copy_kernel(from_ref, to_ref, sem):
+    copy = pltpu.make_async_copy(from_ref, to_ref, sem)
+    copy.start()
+    copy.wait()
+
+
 def merge_kernel(shards, capacity, heads, *refs):
     cache_ref, query_ref, count_ref = refs[:3]
     message_refs = refs[3 : 3 + shards]
-    merged_ref, partial_ref, cache_buf, merged_buf, in_sem, out_sem = refs[3 + shards :]
-    pairs, kept_dev, width = cache_buf.shape
+    merged_ref, partial_ref = refs[3 + shards :]
+    pairs, kept_dev, width = merged_ref.shape
     head_dim = width // 2
     rows_each = query_ref.shape[1]
     slots = shards * capacity
     scale = 1.0 / math.sqrt(head_dim)
-    loads = [
-        pltpu.make_async_copy(cache_ref.at[p], cache_buf.at[p], in_sem.at[p]) for p in range(pairs)
-    ]
-    stores = [
-        pltpu.make_async_copy(merged_buf.at[p], merged_ref.at[p], out_sem.at[p])
-        for p in range(pairs)
-    ]
-    for load in loads:
-        load.start()
     lane = lax.broadcasted_iota(jnp.int32, (pairs, slots), 1)
     weights = jnp.zeros((pairs, slots), jnp.float32)
     positions = jnp.zeros((pairs, slots), jnp.float32)
@@ -96,9 +107,7 @@
             received.append(message_refs[k][0 : pairs * capacity, :].astype(jnp.float32))
     positions = (positions + float(kept_dev // 2)).astype(jnp.int32)
     kept_index = lax.broadcasted_iota(jnp.int32, (kept_dev, slots), 0)
-    column = lax.broadcasted_iota(jnp.int32, (rows_each, kept_dev), 1)
     ones = jnp.ones((slots, head_dim), jnp.bfloat16)
-    tops, totals = [], []
     for p in range(pairs):
         if capacity % 16:
             rows = [r[p * capacity : (p + 1) * capacity] for r in received]
@@ -110,58 +119,71 @@
         placing = placing.astype(jnp.bfloat16)
         summed = dot(placing, rows, ((1,), (0,)))
         share = 1.0 / (1.0 + dot(placing, ones, ((1,), (0,))))
-        loads[p].wait()
-        stored = cache_buf[p].astype(jnp.float32) + summed
-        keys = (stored[:, 0:head_dim] * share).astype(jnp.bfloat16)
-        values = (stored[:, head_dim:] * share).astype(jnp.bfloat16)
-        merged_buf[p, :, 0:head_dim] = keys
-        merged_buf[p, :, head_dim:] = values
-        stores[p].start()
-        scores = dot(query_ref[p], keys, ((1,), (1,))) * scale
-        scores = jnp.where(column < count_ref[p // heads, 0], scores, -1e30)
+        stored = cache_ref[p].astype(jnp.float32) + summed
+        merged_ref[p, :, 0:head_dim] = (stored[:, 0:head_dim] * share).astype(jnp.bfloat16)
+        merged_ref[p, :, head_dim:] = (stored[:, head_dim:] * share).astype(jnp.bfloat16)
+    column = lax.broadcasted_iota(jnp.int32, (heads * rows_each, kept_dev), 1)
+    stat_lane = lax.broadcasted_iota(jnp.int32, (heads * rows_each, head_dim), 1)
+    codes, stats = [], []
+    for r in range(pairs // heads):
+        own = range(r * heads, (r + 1) * heads)
+        scores = [dot(query_ref[p], merged_ref[p, :, 0:head_dim], ((1,), (1,))) for p in own]
+        scores = jnp.concatenate(scores, axis=0) * scale
+        scores = jnp.where(column < count_ref[r, 0], scores, -1e30)
         top = jnp.max(scores, axis=1, keepdims=True)
         exponent = jnp.exp(scores - top)
-        tops.append(top)
-        totals.append(jnp.sum(exponent, axis=1, keepdims=True))
-        partial_ref[p * rows_each : (p + 1) * rows_each, :] = dot(
-            exponent.astype(jnp.bfloat16), values, ((1,), (0,))
-        )
-    stat_lane = lax.broadcasted_iota(jnp.int32, (heads * rows_each, head_dim), 1)
-    stats = []
-    for first in range(0, pairs, heads):
-        top = jnp.concatenate(tops[first : first + heads], axis=0)
-        total = jnp.concatenate(totals[first : first + heads], axis=0)
-        both = jnp.where(stat_lane == 0, top, jnp.where(stat_lane == 1, total, 0.0))
-        stats.append(jnp.transpose(both)[0:2, :])
-    stats.append(jnp.zeros((STAT_ROWS - 2 * (pairs // heads), head_dim), jnp.float32))
-    partial_ref[pairs * rows_each : pairs * rows_each + STAT_ROWS, :] = jnp.concatenate(
-        stats, axis=0
-    )
-    for store in stores:
-        store.wait()
-
-
-def combine_kernel(shards, heads, *refs):
+        total = jnp.sum(exponent, axis=1, keepdims=True)
+        exponent = exponent.astype(jnp.bfloat16)
+        weighted = [
+            dot(
+                exponent[i * rows_each : (i + 1) * rows_each],
+                merged_ref[p, :, head_dim:],
+                ((1,), (0,)),
+            )
+            for i, p in enumerate(own)
+        ]
+        weighted = jnp.concatenate(weighted, axis=0)
+        largest = jnp.max(jnp.abs(weighted), axis=1, keepdims=True)
+        level = jnp.ceil(jnp.log2(jnp.maximum(largest, SMALLEST)) * LEVELS)
+        code = jnp.floor(weighted * (CODE_MAX / jnp.exp2(level / LEVELS)) + 0.5)
+        codes.append(jnp.clip(code, -CODE_MAX, CODE_MAX).astype(jnp.int32))
+        both = jnp.where(stat_lane == 0, top, jnp.where(stat_lane == 1, total, level))
+        both = jnp.transpose(both)
+        top, total, level = both[0:1], both[1:2], both[2:3]
+        whole = jnp.floor(top)
+        stats.append(whole.astype(jnp.int32))
+        stats.append(((top - whole) * FRACTION).astype(jnp.int32))
+        stats.append((total * (FRACTION / kept_dev)).astype(jnp.int32))
+        stats.append(level.astype(jnp.int32))
+    codes = jnp.concatenate(codes, axis=0)
+    half = pairs * rows_each // 2
+    partial_ref[0:half, :] = (codes[0:half] << 16) | (codes[half:] & 0xFFFF)
+    partial_ref[half:, :] = jnp.concatenate(stats, axis=0)
+
+
+def combine_kernel(shards, heads, kept_dev, *refs):
     partial_refs = refs[:shards]
     fresh_top_ref, fresh_total_ref, fresh_ref, out_ref, ordered = refs[shards:]
     steps, requests, query_local, head_dim = out_ref.shape
     group = query_local // heads
     rows_each = steps * group
     rows_request = heads * rows_each
+    half = requests * rows_request // 2
     me = lax.axis_index("seq")
     for k in range(shards):
         source = jnp.where(me >= k, me - k, me - k + shards)
         ordered[source] = partial_refs[k][...]
     for r in range(requests):
-        tops, totals = [fresh_top_ref[r : r + 1, :]], [fresh_total_ref[r : r + 1, :]]
+        tops, totals, units = [fresh_top_ref[r : r + 1, :]], [fresh_total_ref[r : r + 1, :]], [1.0]
         for b in range(shards):
-            first = requests * rows_request + 2 * r
-            tops.append(ordered[b, first : first + 1, :])
-            totals.append(ordered[b, first + 1 : first + 2, :])
+            stats = ordered[b, half + r * STATS : half + (r + 1) * STATS, :].astype(jnp.float32)
+            tops.append(stats[0:1] + stats[1:2] * (1.0 / FRACTION))
+            totals.append(stats[2:3] * (kept_dev / FRACTION))
+            units.append(jnp.exp2(stats[3:4] / LEVELS) * (1.0 / CODE_MAX))
         highest = functools.reduce(jnp.maximum, tops)
         scales = [jnp.exp(top - highest) for top in tops]
         total = sum(a * b for a, b in zip(totals, scales))
-        factors = jnp.concatenate([s / total for s in scales], axis=0)
+        factors = jnp.concatenate([s * u / total for s, u in zip(scales, units)], axis=0)
         padding = -(shards + 1) % 8
         if padding:
             factors = jnp.concatenate(
@@ -170,8 +192,11 @@
         factors = jnp.transpose(factors)
         first = r * rows_request
         result = fresh_ref[first : first + rows_request, :] * factors[:, 0:1]
+        low = first % half
         for b in range(shards):
-            result += ordered[b, first : first + rows_request, :] * factors[:, b + 1 : b + 2]
+            words = ordered[b, low : low + rows_request, :]
+            codes = words >> 16 if first < half else (words << 16) >> 16
+            result += codes.astype(jnp.float32) * factors[:, b + 1 : b + 2]
         for s in range(steps):
             pieces = [
                 result[h * rows_each + s * group : h * rows_each + (s + 1) * group]
@@ -212,20 +237,30 @@
     vmem = pl.BlockSpec(memory_space=pltpu.VMEM)
     smem = pl.BlockSpec(memory_space=pltpu.SMEM)
     anywhere = pl.BlockSpec(memory_space=pl.ANY)
+
+    def in_hbm(array):
+        return pltpu.with_memory_space_constraint(array, pltpu.HBM)
+
     params = pltpu.CompilerParams(vmem_limit_bytes=VMEM_BYTES)
 
     message = jax.ShapeDtypeStruct((pairs * capacity + META_ROWS, width), jnp.bfloat16)
     messages = pl.pallas_call(
         functools.partial(pack_kernel, shards, capacity, kept_dev),
         out_shape=[message] * shards,
-        in_specs=[vmem] * 3,
+        in_specs=[anywhere] * 3,
         out_specs=[vmem] * shards,
+        scratch_shapes=[
+            pltpu.VMEM((pairs, evict_dev, width), jnp.bfloat16),
+            pltpu.VMEM((pairs, evict_dev), jnp.bfloat16),
+            pltpu.VMEM((pairs, evict_dev), jnp.int32),
+            pltpu.SemaphoreType.DMA((3,)),
+        ],
         compiler_params=params,
         name="pack",
     )(
-        evicted.reshape(pairs, evict_dev, width),
-        merge_weight.reshape(pairs, evict_dev),
-        targets.reshape(pairs, evict_dev),
+        in_hbm(evicted.reshape(pairs, evict_dev, width)),
+        in_hbm(merge_weight.reshape(pairs, evict_dev)),
+        in_hbm(targets.reshape(pairs, evict_dev)),
     )
 
     def shifted(array, k):
@@ -238,32 +273,48 @@
     fresh_rows = new_rows.transpose(1, 2, 0, 3).reshape(pairs, steps, width)
     fresh_top, fresh_total, fresh = fresh_block(query_rows, fresh_rows, group)
 
+    staged = pl.pallas_call(
+        copy_kernel,
+        out_shape=jax.ShapeDtypeStruct((pairs, kept_dev, width), jnp.bfloat16),
+        in_specs=[anywhere],
+        out_specs=vmem,
+        scratch_shapes=[pltpu.SemaphoreType.DMA],
+        compiler_params=params,
+        name="stage",
+    )(in_hbm(cache.reshape(pairs, kept_dev, width)))
+
+    half = pairs * rows_each // 2
     merged, partial = pl.pallas_call(
         functools.partial(merge_kernel, shards, capacity, head_local),
         out_shape=[
             jax.ShapeDtypeStruct((pairs, kept_dev, width), jnp.bfloat16),
-            jax.ShapeDtypeStruct((pairs * rows_each + STAT_ROWS, head_dim), jnp.float32),
+            jax.ShapeDtypeStruct((half + STATS * req_local, head_dim), jnp.int32),
         ],
-        in_specs=[anywhere, vmem, smem] + [vmem] * shards,
-        out_specs=[anywhere, vmem],
-        scratch_shapes=[
-            pltpu.VMEM((pairs, kept_dev, width), jnp.bfloat16),
-            pltpu.VMEM((pairs, kept_dev, width), jnp.bfloat16),
-            pltpu.SemaphoreType.DMA((pairs,)),
-            pltpu.SemaphoreType.DMA((pairs,)),
-        ],
+        in_specs=[vmem, vmem, smem] + [vmem] * shards,
+        out_specs=[vmem, vmem],
+        input_output_aliases={0: 0},
         compiler_params=params,
         name="merge",
-    )(cache.reshape(pairs, kept_dev, width), query_rows, kept_counts, *messages)
+    )(staged, query_rows, kept_counts, *messages)
 
     partials = [partial] + [shifted(partial, k) for k in range(shards - 1, 0, -1)][::-1]
 
+    merged = pl.pallas_call(
+        copy_kernel,
+        out_shape=pltpu.HBM((pairs, kept_dev, width), jnp.bfloat16),
+        in_specs=[vmem],
+        out_specs=anywhere,
+        scratch_shapes=[pltpu.SemaphoreType.DMA],
+        compiler_params=params,
+        name="unstage",
+    )(merged)
+
     attended = pl.pallas_call(
-        functools.partial(combine_kernel, shards, head_local),
+        functools.partial(combine_kernel, shards, head_local, kept_dev),
         out_shape=jax.ShapeDtypeStruct(queries.shape, jnp.bfloat16),
         in_specs=[vmem] * (shards + 3),
         out_specs=vmem,
-        scratch_shapes=[pltpu.VMEM((shards,) + partial.shape, jnp.float32)],
+        scratch_shapes=[pltpu.VMEM((shards,) + partial.shape, jnp.int32)],
         compiler_params=params,
         name="combine",
     )(

time: 42.7 us -> 31.4 us (0.74)
  the two profiles are of different devices: /device:TPU:13 before, /device:TPU:0 now
where the time goes in v2:
time: 31.4 us; the launch traced here: 31.2 us
  starting transfers between devices  12.9 us (41%)
  waiting for transfers between devices  8.25 us (26%)
  Pallas kernels  7.74 us (25%)
  local copies, waits for them, and re-layouts  1.12 us (4%)
  between operations  0.72 us (2%)
  matrix products  0.37 us (1%)
    ppermute x6, starting transfers between devices, shifted(): lax.ppermute(array, 'seq', [(i, (i + k) % shards) for i in range(shards)])  12.9 us
    ppermute x6, waiting for transfers between devices, shifted(): lax.ppermute(array, 'seq', [(i, (i + k) % shards) for i in range(shards)])  8.25 us
    pallas_call x1, Pallas kernels, body(): pl.pallas_call(functools.partial(merge_kernel, shards, capacity, head_loc...  2.61 us
    pallas_call x1, Pallas kernels, body(): pl.pallas_call(copy_kernel, out_shape=jax.ShapeDtypeStruct((pairs, kept_d...  1.43 us
    pallas_call x1, Pallas kernels, body(): pl.pallas_call(functools.partial(pack_kernel, shards, capacity, kept_dev)...  1.41 us
    pallas_call x1, Pallas kernels, body(): pl.pallas_call(copy_kernel, out_shape=pltpu.HBM((pairs, kept_dev, width),...  1.15 us
    pallas_call x1, Pallas kernels, body(): pl.pallas_call(functools.partial(combine_kernel, shards, head_local, kept...  1.14 us
    reshape x1, local copies, waits for them, and re-layouts, body(): query_rows = queries.reshape(steps, req_local, head_local, group, head_dim)  0.85 us
  transfers between devices with their start and end apart: 6, of which 4 were waited for; matrix products, arithmetic and copies ran while one was open for 5% of the time, Pallas kernels for 8%

profile of v2, /device:TPU:0, one launch (start us, length us, event | category | flops | bytes accessed | tf_op | source)
XLA Modules:
  0.0 31.2 jit_solution(7448749338726182668)
XLA Ops:
  0.6 1.4 %pack.1 = (bf16[272,256]{1,0:T(8,128)(2,1)S(1)}, bf16[272,256]{1,0:T(8,128)(2,1)S(1)}, bf16[272,256]{1,0:T(8,128)(2,1)S(1)}, bf16[272,256]{1,0:T(8,128)(2,1)S(1)}) custom-call(bf16[8,64,256]{2,1,0:T(8,128)(2,1)} %bitcast.18, bf16[8,64]{1,0:T(8,128)(2,1)} %bitcast.24, s32[8,64]{1,0:T(8,128)} %bitcast.23), custom_call_target="tpu_custom_call" | custom-call | tf_op jit(solution)/shard_map/pack/pallas_call | solution.py:247
  2.0 3.1 %collective-permute-start = (bf16[272,256]{1,0:T(8,128)(2,1)S(1)}, bf16[272,256]{1,0:T(8,128)(2,1)S(1)}, u32[]{:S(2)}, u32[]{:S(2)}) collective-permute-start(bf16[272,256]{1,0:T(8,128)(2,1)S(1)} %get-tuple-element.9), channel_id=1, source_target_pairs={{0,4},{4,8},{8,12},{12,0},{1,5},{5,9},{9,13},{13,1},{2,6},{6,10},{... | collective-permute-start | bytes 417800 | tf_op jit(solution)/shard_map/ppermute | solution.py:267
  5.1 2.6 %collective-permute-start.1 = (bf16[272,256]{1,0:T(8,128)(2,1)S(1)}, bf16[272,256]{1,0:T(8,128)(2,1)S(1)}, u32[]{:S(2)}, u32[]{:S(2)}) collective-permute-start(bf16[272,256]{1,0:T(8,128)(2,1)S(1)} %get-tuple-element.10), channel_id=1, source_target_pairs={{0,8},{4,12},{8,0},{12,4},{1,9},{5,13},{9,1},{13,5},{2,10},{6,14},... | collective-permute-start | bytes 417800 | tf_op jit(solution)/shard_map/ppermute | solution.py:267
  7.7 1.3 %collective-permute-start.2 = (bf16[272,256]{1,0:T(8,128)(2,1)S(1)}, bf16[272,256]{1,0:T(8,128)(2,1)S(1)}, u32[]{:S(2)}, u32[]{:S(2)}) collective-permute-start(bf16[272,256]{1,0:T(8,128)(2,1)S(1)} %get-tuple-element.11), channel_id=1, source_target_pairs={{0,12},{4,0},{8,4},{12,8},{1,13},{5,1},{9,5},{13,9},{2,14},{6,2},{... | collective-permute-start | bytes 417800 | tf_op jit(solution)/shard_map/ppermute | solution.py:267
  9.1 0.9 %copy.10 = bf16[4,2,4,8,128]{4,3,0,2,1:T(8,128)(2,1)S(1)} copy(bf16[4,2,4,8,128]{4,3,2,1,0:T(8,128)(2,1)} %bitcast.19) | data formatting | bytes 131072 | tf_op jit(solution)/shard_map/reshape | solution.py:271
  9.9 0.0 copy-start.1
  9.9 0.0 copy-start
  9.9 1.4 %stage.1.refs_0_ = bf16[8,384,256]{2,1,0:T(8,128)(2,1)S(1)} custom-call(bf16[8,384,256]{2,1,0:T(8,128)(2,1)} %bitcast.16), custom_call_target="tpu_custom_call" | custom-call | tf_op jit(solution)/shard_map/stage/pallas_call | solution.py:276
  11.4 0.1 copy.11.refs_2_
  11.5 0.2 fusion.8
  11.7 0.1 reshape.78.refs_4_
  11.7 0.2 fusion.3
  12.0 0.0 collective-permute-done.refs_4_
  12.0 4.9 %collective-permute-done.1.refs_5_ = bf16[272,256]{1,0:T(8,128)(2,1)S(1)} collective-permute-done((bf16[272,256]{1,0:T(8,128)(2,1)S(1)}, bf16[272,256]{1,0:T(8,128)(2,1)S(1)}, u32[]{:S(2)}, u32[]{:S(2)}) %collective-permute-start.1) | collective-permute-done | bytes 139296 | tf_op jit(solution)/shard_map/ppermute | solution.py:267
  16.9 2.6 %merge.1 = (bf16[8,384,256]{2,1,0:T(8,128)(2,1)S(1)}, s32[136,128]{1,0:T(8,128)S(1)}) custom-call(bf16[8,384,256]{2,1,0:T(8,128)(2,1)S(1)} %stage.1.refs_0_, bf16[8,32,128]{2,1,0:T(8,128)(2,1)S(1)} %bitcast.15, s32[2,1]{1,0:T(2,128)S(1)} %copy.11.refs_2_, bf16[272,256]{1,0:T(8,128)(2,1)S(1)} %get-tuple-element.8.refs_3_, ...), custom_call_target="tpu_custom_call", output_to_operand_aliasing={{0}: (0, {})} | custom-call | tf_op jit(solution)/shard_map/merge/pallas_call | solution.py:287
  19.5 3.5 %collective-permute-start.3 = (s32[136,128]{1,0:T(8,128)S(1)}, s32[136,128]{1,0:T(8,128)S(1)}, u32[]{:S(2)}, u32[]{:S(2)}) collective-permute-start(s32[136,128]{1,0:T(8,128)S(1)} %get-tuple-element.13.refs_0_), channel_id=1, source_target_pairs={{0,4},{4,8},{8,12},{12,0},{1,5},{5,9},{9,13},{13,1},{2,6},{6,10},{... | collective-permute-start | bytes 208904 | tf_op jit(solution)/shard_map/ppermute | solution.py:267
  23.0 1.6 %collective-permute-start.4 = (s32[136,128]{1,0:T(8,128)S(1)}, s32[136,128]{1,0:T(8,128)S(1)}, u32[]{:S(2)}, u32[]{:S(2)}) collective-permute-start(s32[136,128]{1,0:T(8,128)S(1)} %get-tuple-element.13.refs_0_), channel_id=1, source_target_pairs={{0,8},{4,12},{8,0},{12,4},{1,9},{5,13},{9,1},{13,5},{2,10},{6,14},... | collective-permute-start | bytes 208904 | tf_op jit(solution)/shard_map/ppermute | solution.py:267
  24.6 0.8 %collective-permute-start.5 = (s32[136,128]{1,0:T(8,128)S(1)}, s32[136,128]{1,0:T(8,128)S(1)}, u32[]{:S(2)}, u32[]{:S(2)}) collective-permute-start(s32[136,128]{1,0:T(8,128)S(1)} %get-tuple-element.13.refs_0_), channel_id=1, source_target_pairs={{0,12},{4,0},{8,4},{12,8},{1,13},{5,1},{9,5},{13,9},{2,14},{6,2},{... | collective-permute-start | bytes 208904 | tf_op jit(solution)/shard_map/ppermute | solution.py:267
  25.5 0.1 reshape.79.refs_5_
  25.5 1.2 %unstage.1 = bf16[8,384,256]{2,1,0:T(8,128)(2,1)} custom-call(bf16[8,384,256]{2,1,0:T(8,128)(2,1)S(1)} %get-tuple-element.12.from_ref), custom_call_target="tpu_custom_call" | custom-call | tf_op jit(solution)/shard_map/unstage/pallas_call | solution.py:302
  26.7 0.1 collective-permute-done.3.refs_1_
  26.8 2.6 %collective-permute-done.4.refs_2_ = s32[136,128]{1,0:T(8,128)S(1)} collective-permute-done((s32[136,128]{1,0:T(8,128)S(1)}, s32[136,128]{1,0:T(8,128)S(1)}, u32[]{:S(2)}, u32[]{:S(2)}) %collective-permute-start.4) | collective-permute-done | bytes 69664 | tf_op jit(solution)/shard_map/ppermute | solution.py:267
  29.4 0.6 %collective-permute-done.5.refs_3_ = s32[136,128]{1,0:T(8,128)S(1)} collective-permute-done((s32[136,128]{1,0:T(8,128)S(1)}, s32[136,128]{1,0:T(8,128)S(1)}, u32[]{:S(2)}, u32[]{:S(2)}) %collective-permute-start.5) | collective-permute-done | bytes 69664 | tf_op jit(solution)/shard_map/ppermute | solution.py:267
  30.0 1.1 %combine.1 = bf16[4,2,32,128]{3,2,1,0:T(8,128)(2,1)} custom-call(s32[136,128]{1,0:T(8,128)S(1)} %get-tuple-element.13.refs_0_, s32[136,128]{1,0:T(8,128)S(1)} %collective-permute-done.3.refs_1_, s32[136,128]{1,0:T(8,128)S(1)} %collective-permute-done.4.refs_2_, s32[136,128]{1,0:T(8,128)S(1)} %collective-permute-done.5.refs_3_, ...), custom_call_target="tpu_custom_call" | custom-call | tf_op jit(solution)/shard_map/combine/pallas_call | solution.py:312
  (7 shorter events, 0.0 us)
Async XLA Ops:
  2.0 9.9 %collective-permute-start = (bf16[272,256]{1,0:T(8,128)(2,1)S(1)}, bf16[272,256]{1,0:T(8,128)(2,1)S(1)}, u32[]{:S(2)}, u32[]{:S(2)}) collective-permute-start(bf16[272,256]{1,0:T(8,128)(2,1)S(1)} %get-tuple-element.9), channel_id=1, source_target_pairs={{0,4},{4,8},{8,12},{12,0},{1,5},{5,9},{9,13},{13,1},{2,6},{6,10},{... | collective-permute-start | bytes 417800 | tf_op jit(solution)/shard_map/ppermute | solution.py:267
  5.1 11.8 %collective-permute-start.1 = (bf16[272,256]{1,0:T(8,128)(2,1)S(1)}, bf16[272,256]{1,0:T(8,128)(2,1)S(1)}, u32[]{:S(2)}, u32[]{:S(2)}) collective-permute-start(bf16[272,256]{1,0:T(8,128)(2,1)S(1)} %get-tuple-element.10), channel_id=1, source_target_pairs={{0,8},{4,12},{8,0},{12,4},{1,9},{5,13},{9,1},{13,5},{2,10},{6,14},... | collective-permute-start | bytes 417800 | tf_op jit(solution)/shard_map/ppermute | solution.py:267
  7.7 9.2 %collective-permute-start.2 = (bf16[272,256]{1,0:T(8,128)(2,1)S(1)}, bf16[272,256]{1,0:T(8,128)(2,1)S(1)}, u32[]{:S(2)}, u32[]{:S(2)}) collective-permute-start(bf16[272,256]{1,0:T(8,128)(2,1)S(1)} %get-tuple-element.11), channel_id=1, source_target_pairs={{0,12},{4,0},{8,4},{12,8},{1,13},{5,1},{9,5},{13,9},{2,14},{6,2},{... | collective-permute-start | bytes 417800 | tf_op jit(solution)/shard_map/ppermute | solution.py:267
  9.9 1.5 %copy-start.1 = (s32[2,1]{0,1:T(1,128)S(1)}, s32[2,1]{0,1:T(1,128)}, u32[]{:S(2)}) copy-start(s32[2,1]{0,1:T(1,128)} %param.11) | copy-start | bytes 28
  9.9 1.6 %copy-start = (bf16[4,2,4,256]{3,2,1,0:T(4,128)(2,1)S(1)}, bf16[4,2,4,256]{3,2,1,0:T(4,128)(2,1)}, u32[]{:S(2)}) copy-start(bf16[4,2,4,256]{3,2,1,0:T(4,128)(2,1)} %param.13) | copy-start | bytes 49156
  19.5 7.3 %collective-permute-start.3 = (s32[136,128]{1,0:T(8,128)S(1)}, s32[136,128]{1,0:T(8,128)S(1)}, u32[]{:S(2)}, u32[]{:S(2)}) collective-permute-start(s32[136,128]{1,0:T(8,128)S(1)} %get-tuple-element.13.refs_0_), channel_id=1, source_target_pairs={{0,4},{4,8},{8,12},{12,0},{1,5},{5,9},{9,13},{13,1},{2,6},{6,10},{... | collective-permute-start | bytes 208904 | tf_op jit(solution)/shard_map/ppermute | solution.py:267
  23.0 6.4 %collective-permute-start.4 = (s32[136,128]{1,0:T(8,128)S(1)}, s32[136,128]{1,0:T(8,128)S(1)}, u32[]{:S(2)}, u32[]{:S(2)}) collective-permute-start(s32[136,128]{1,0:T(8,128)S(1)} %get-tuple-element.13.refs_0_), channel_id=1, source_target_pairs={{0,8},{4,12},{8,0},{12,4},{1,9},{5,13},{9,1},{13,5},{2,10},{6,14},... | collective-permute-start | bytes 208904 | tf_op jit(solution)/shard_map/ppermute | solution.py:267
  24.6 5.4 %collective-permute-start.5 = (s32[136,128]{1,0:T(8,128)S(1)}, s32[136,128]{1,0:T(8,128)S(1)}, u32[]{:S(2)}, u32[]{:S(2)}) collective-permute-start(s32[136,128]{1,0:T(8,128)S(1)} %get-tuple-element.13.refs_0_), channel_id=1, source_target_pairs={{0,12},{4,0},{8,4},{12,8},{1,13},{5,1},{9,5},{13,9},{2,14},{6,2},{... | collective-permute-start | bytes 208904 | tf_op jit(solution)/shard_map/ppermute | solution.py:267

commit v3 on v2

v3 whole, which is shorter than its diff:
```python
import functools
import math

import jax
import jax.numpy as jnp
from jax import lax
from jax.experimental import pallas as pl
from jax.experimental.pallas import tpu as pltpu
from jax.sharding import PartitionSpec as P

META_ROWS = 8
STATS = 4
CODE_MAX = 32767.0
LEVELS = 16.0
SMALLEST = 1e-36
FRACTION = 2.0**30
VMEM_BYTES = 8 * 1024 * 1024


def dot(a, b, contract):
    return lax.dot_general(a, b, (contract, ((), ())), preferred_element_type=jnp.float32)


def pack_kernel(shards, capacity, kept_dev, requests, plan, *refs):
    message_refs = refs[3 : 3 + len(plan)]
    evicted_ref, weight_ref, target_ref, sems = refs[3 + len(plan) :]
    loads = [
        pltpu.make_async_copy(refs[i], refs[3 + len(plan) + i], sems.at[i]) for i in (2, 1, 0)
    ]
    for load in loads:
        load.start()
    pairs, evict_dev, width = evicted_ref.shape
    heads = pairs // requests
    slots = shards * capacity
    me = lax.axis_index("seq")
    loads[0].wait()
    loads[1].wait()
    targets = target_ref[...]
    holder = jnp.zeros_like(targets)
    for block in range(1, shards):
        holder += (targets >= block * kept_dev).astype(jnp.int32)
    centred = targets - holder * kept_dev - kept_dev // 2
    distance = jnp.where(holder >= me, holder - me, holder - me + shards)
    owned = jnp.concatenate(
        [(distance == k).astype(jnp.float32) for k in range(shards)], axis=0
    )
    before = lax.broadcasted_iota(jnp.int32, (evict_dev, evict_dev), 0) < lax.broadcasted_iota(
        jnp.int32, (evict_dev, evict_dev), 1
    )
    prefix = dot(owned.astype(jnp.bfloat16), before.astype(jnp.bfloat16), ((1,), (0,)))
    ranked = owned * prefix
    rank = ranked[0:pairs]
    for k in range(1, shards):
        rank += ranked[k * pairs : (k + 1) * pairs]
    slot = distance * capacity + rank.astype(jnp.int32)
    facts = jnp.concatenate(
        [weight_ref[...].astype(jnp.float32), centred.astype(jnp.float32)], axis=0
    ).astype(jnp.bfloat16)
    slot_index = lax.broadcasted_iota(jnp.int32, (slots, evict_dev), 0)
    meta_index = lax.broadcasted_iota(jnp.int32, (META_ROWS, slots), 0)
    loads[2].wait()
    rows, metas = [], []
    for r in range(requests):
        weights = jnp.zeros((META_ROWS, slots), jnp.float32)
        positions = jnp.zeros((META_ROWS, slots), jnp.float32)
        for h in range(heads):
            p = r * heads + h
            placing = (slot_index == slot[p : p + 1, :]).astype(jnp.float32).astype(jnp.bfloat16)
            rows.append(dot(placing, evicted_ref[p], ((1,), (0,))))
            placed = dot(facts, placing, ((1,), (1,)))
            weights = jnp.where(meta_index == h, placed[p : p + 1], weights)
            positions = jnp.where(meta_index == h, placed[pairs + p : pairs + p + 1], positions)
        metas.append(jnp.concatenate([weights, positions], axis=1))
    for message_ref, (k, members) in zip(message_refs, plan):
        message = [
            rows[r * heads + h][k * capacity : (k + 1) * capacity]
            for r in members
            for h in range(heads)
        ]
        message += [metas[r] for r in members]
        message_ref[...] = jnp.concatenate(message, axis=0).astype(jnp.bfloat16)


def load_kernel(from_ref, *refs):
    to_refs, sems = refs[:-1], refs[-1]
    each = to_refs[0].shape[0]
    copies = [
        pltpu.make_async_copy(from_ref.at[pl.ds(r * each, each)], to_ref, sems.at[r])
        for r, to_ref in enumerate(to_refs)
    ]
    for copy in copies:
        copy.start()
    for copy in copies:
        copy.wait()


def store_kernel(*refs):
    from_refs, to_ref, sems = refs[:-2], refs[-2], refs[-1]
    each = from_refs[0].shape[0]
    copies = [
        pltpu.make_async_copy(from_ref, to_ref.at[pl.ds(r * each, each)], sems.at[r])
        for r, from_ref in enumerate(from_refs)
    ]
    for copy in copies:
        copy.start()
    for copy in copies:
        copy.wait()


def merge_kernel(shards, capacity, request, places, *refs):
    cache_ref, query_ref, count_ref = refs[:3]
    message_refs = refs[3 : 3 + shards]
    before_refs, merged_ref, partial_ref = refs[3 + shards : -2], refs[-2], refs[-1]
    heads, kept_dev, width = merged_ref.shape
    head_dim = width // 2
    rows_each = query_ref.shape[1]
    slots = shards * capacity
    scale = 1.0 / math.sqrt(head_dim)
    lane = lax.broadcasted_iota(jnp.int32, (META_ROWS, slots), 1)
    weights = jnp.zeros((META_ROWS, slots), jnp.float32)
    positions = jnp.zeros((META_ROWS, slots), jnp.float32)
    received = []
    for k in range(shards):
        members, place = places[k]
        first = members * heads * capacity
        meta = message_refs[k][first : first + members * META_ROWS, :].astype(jnp.float32)
        meta = meta[place * META_ROWS : (place + 1) * META_ROWS]
        mine = jnp.logical_and(lane >= k * capacity, lane < (k + 1) * capacity)
        weights = jnp.where(mine, meta[:, 0:slots], weights)
        positions = jnp.where(mine, meta[:, slots : 2 * slots], positions)
        if capacity % 16:
            received.append(message_refs[k][...].astype(jnp.float32))
    positions = (positions + float(kept_dev // 2)).astype(jnp.int32)
    kept_index = lax.broadcasted_iota(jnp.int32, (kept_dev, slots), 0)
    ones = jnp.ones((slots, head_dim), jnp.bfloat16)
    for h in range(heads):
        if capacity % 16:
            rows = [
                m[(place * heads + h) * capacity : (place * heads + h + 1) * capacity]
                for m, (_, place) in zip(received, places)
            ]
            rows = jnp.concatenate(rows, axis=0).astype(jnp.bfloat16)
        else:
            rows = [
                m[(place * heads + h) * capacity : (place * heads + h + 1) * capacity, :]
                for m, (_, place) in zip(message_refs, places)
            ]
            rows = jnp.concatenate(rows, axis=0)
        placing = jnp.where(kept_index == positions[h : h + 1, :], weights[h : h + 1, :], 0.0)
        placing = placing.astype(jnp.bfloat16)
        summed = dot(placing, rows, ((1,), (0,)))
        share = 1.0 / (1.0 + dot(placing, ones, ((1,), (0,))))
        stored = cache_ref[h].astype(jnp.float32) + summed
        merged_ref[h, :, 0:head_dim] = (stored[:, 0:head_dim] * share).astype(jnp.bfloat16)
        merged_ref[h, :, head_dim:] = (stored[:, head_dim:] * share).astype(jnp.bfloat16)
    scores = [
        dot(query_ref[request * heads + h], merged_ref[h, :, 0:head_dim], ((1,), (1,)))
        for h in range(heads)
    ]
    scores = jnp.concatenate(scores, axis=0) * scale
    column = lax.broadcasted_iota(jnp.int32, scores.shape, 1)
    scores = jnp.where(column < count_ref[request : request + 1, :], scores, -1e30)
    top = jnp.max(scores, axis=1, keepdims=True)
    exponent = jnp.exp(scores - top)
    total = jnp.sum(exponent, axis=1, keepdims=True)
    exponent = exponent.astype(jnp.bfloat16)
    weighted = [
        dot(
            exponent[h * rows_each : (h + 1) * rows_each],
            merged_ref[h, :, head_dim:],
            ((1,), (0,)),
        )
        for h in range(heads)
    ]
    weighted = jnp.concatenate(weighted, axis=0)
    largest = jnp.max(jnp.abs(weighted), axis=1, keepdims=True)
    level = jnp.ceil(jnp.log2(jnp.maximum(largest, SMALLEST)) * LEVELS)
    codes = jnp.floor(weighted * (CODE_MAX / jnp.exp2(level / LEVELS)) + 0.5)
    codes = jnp.clip(codes, -CODE_MAX, CODE_MAX).astype(jnp.int32)
    stat_lane = lax.broadcasted_iota(jnp.int32, weighted.shape, 1)
    stats = jnp.where(stat_lane == 0, top, jnp.where(stat_lane == 1, total, level))
    stats = jnp.transpose(stats)
    top, total, level = stats[0:1], stats[1:2], stats[2:3]
    whole = jnp.floor(top)
    half = heads * rows_each // 2
    words = (codes[0:half] << 16) | (codes[half:] & 0xFFFF)
    stats = [
        whole.astype(jnp.int32),
        ((top - whole) * FRACTION).astype(jnp.int32),
        (total * (FRACTION / kept_dev)).astype(jnp.int32),
        level.astype(jnp.int32),
    ]
    for i, before_ref in enumerate(before_refs):
        partial_ref[i * half : (i + 1) * half, :] = before_ref[0:half, :]
    stats = [before_ref[half : half + STATS, :] for before_ref in before_refs] + stats
    filler = -STATS * (len(before_refs) + 1) % 8
    if filler:
        stats.append(jnp.zeros((filler, top.shape[1]), jnp.int32))
    first = len(before_refs) * half
    partial_ref[first : first + half, :] = words
    partial_ref[first + half :, :] = jnp.concatenate(stats, axis=0)


def combine_kernel(shards, heads, kept_dev, *refs):
    partial_refs = refs[:shards]
    fresh_top_ref, fresh_total_ref, fresh_ref, out_ref, ordered = refs[shards:]
    steps, requests, query_local, head_dim = out_ref.shape
    group = query_local // heads
    rows_each = steps * group
    rows_request = heads * rows_each
    half = rows_request // 2
    me = lax.axis_index("seq")
    for k in range(shards):
        source = jnp.where(me >= k, me - k, me - k + shards)
        ordered[source] = partial_refs[k][...]
    for r in range(requests):
        tops, totals, units = [fresh_top_ref[r : r + 1, :]], [fresh_total_ref[r : r + 1, :]], [1.0]
        for b in range(shards):
            stats = ordered[b, requests * half : requests * (half + STATS), :].astype(jnp.float32)
            stats = stats[r * STATS : (r + 1) * STATS]
            tops.append(stats[0:1] + stats[1:2] * (1.0 / FRACTION))
            totals.append(stats[2:3] * (kept_dev / FRACTION))
            units.append(jnp.exp2(stats[3:4] / LEVELS) * (1.0 / CODE_MAX))
        highest = functools.reduce(jnp.maximum, tops)
        scales = [jnp.exp(top - highest) for top in tops]
        total = sum(a * b for a, b in zip(totals, scales))
        factors = jnp.concatenate([s * u / total for s, u in zip(scales, units)], axis=0)
        padding = -(shards + 1) % 8
        if padding:
            factors = jnp.concatenate(
                [factors, jnp.zeros((padding, rows_request), jnp.float32)], axis=0
            )
        factors = jnp.transpose(factors)
        first = r * rows_request
        result = fresh_ref[first : first + rows_request, :] * factors[:, 0:1]
        for b in range(shards):
            words = ordered[b, r * half : (r + 1) * half, :]
            codes = jnp.concatenate([words >> 16, (words << 16) >> 16], axis=0)
            result += codes.astype(jnp.float32) * factors[:, b + 1 : b + 2]
        for s in range(steps):
            pieces = [
                result[h * rows_each + s * group : h * rows_each + (s + 1) * group]
                for h in range(heads)
            ]
            out_ref[s, r] = jnp.concatenate(pieces, axis=0).astype(jnp.bfloat16)


def fresh_block(query_rows, fresh_rows, group):
    head_dim = query_rows.shape[-1]
    scores = jnp.einsum(
        "pqd,pjd->pqj", query_rows, fresh_rows[..., :head_dim], preferred_element_type=jnp.float32
    ) * (1.0 / math.sqrt(head_dim))
    step_index = jnp.arange(query_rows.shape[1], dtype=jnp.int32) // group
    allowed = jnp.arange(fresh_rows.shape[1], dtype=jnp.int32)[None, :] <= step_index[:, None]
    scores = jnp.where(allowed[None], scores, -1e30)
    top = jnp.max(scores, axis=-1)
    exponent = jnp.exp(scores - top[..., None])
    weighted = jnp.einsum(
        "pqj,pjd->pqd",
        exponent.astype(jnp.bfloat16),
        fresh_rows[..., head_dim:],
        preferred_element_type=jnp.float32,
    )
    return (top, jnp.sum(exponent, axis=-1), weighted)


def body(cache, evicted, merge_weight, targets, kept_counts, queries, new_rows):
    req_local, head_local, kept_dev, width = cache.shape
    head_dim = width // 2
    shards = lax.axis_size("seq")
    evict_dev = evicted.shape[2]
    capacity = max(2, 2 * evict_dev // shards)
    pairs = req_local * head_local
    steps, _, query_local, _ = queries.shape
    group = query_local // head_local
    rows_each = steps * group
    vmem = pl.BlockSpec(memory_space=pltpu.VMEM)
    anywhere = pl.BlockSpec(memory_space=pl.ANY)

    def in_hbm(array):
        return pltpu.with_memory_space_constraint(array, pltpu.HBM)

    params = pltpu.CompilerParams(vmem_limit_bytes=VMEM_BYTES)

    rows_request = head_local * rows_each
    every = tuple(range(req_local))
    plan = [(k, every) for k in range(min(2, shards))]
    plan += [(k, (r,)) for r in every for k in range(2, shards)]
    packed = pl.pallas_call(
        functools.partial(pack_kernel, shards, capacity, kept_dev, req_local, plan),
        out_shape=[
            jax.ShapeDtypeStruct(
                (len(m) * (head_local * capacity + META_ROWS), width), jnp.bfloat16
            )
            for _, m in plan
        ],
        in_specs=[anywhere] * 3,
        out_specs=[vmem] * len(plan),
        scratch_shapes=[
            pltpu.VMEM((pairs, evict_dev, width), jnp.bfloat16),
            pltpu.VMEM((pairs, evict_dev), jnp.bfloat16),
            pltpu.VMEM((pairs, evict_dev), jnp.int32),
            pltpu.SemaphoreType.DMA((3,)),
        ],
        compiler_params=params,
        name="pack",
    )(
        in_hbm(evicted.reshape(pairs, evict_dev, width)),
        in_hbm(merge_weight.reshape(pairs, evict_dev)),
        in_hbm(targets.reshape(pairs, evict_dev)),
    )

    def shifted(array, k):
        return lax.ppermute(array, "seq", [(i, (i + k) % shards) for i in range(shards)])

    messages = [shifted(m, k) if k else m for m, (k, _) in zip(packed, plan)]

    query_rows = queries.reshape(steps, req_local, head_local, group, head_dim)
    query_rows = query_rows.transpose(1, 2, 0, 3, 4).reshape(pairs, rows_each, head_dim)
    fresh_rows = new_rows.transpose(1, 2, 0, 3).reshape(pairs, steps, width)
    fresh_top, fresh_total, fresh = fresh_block(query_rows, fresh_rows, group)
    fresh_top = fresh_top.reshape(req_local, rows_request)
    fresh_total = fresh_total.reshape(req_local, rows_request)
    fresh = fresh.reshape(pairs * rows_each, head_dim)

    block = jax.ShapeDtypeStruct((head_local, kept_dev, width), jnp.bfloat16)
    staged = pl.pallas_call(
        load_kernel,
        out_shape=[block] * req_local,
        in_specs=[anywhere],
        out_specs=[vmem] * req_local,
        scratch_shapes=[pltpu.SemaphoreType.DMA((req_local,))],
        compiler_params=params,
        name="stage",
    )(in_hbm(cache.reshape(pairs, kept_dev, width)))

    merged, partials = [], []
    for r in range(req_local):
        last = r == req_local - 1
        mine = [i for i, (_, m) in enumerate(plan) if r in m]
        places = [(len(plan[i][1]), plan[i][1].index(r)) for i in mine]
        parts = req_local if last else 1
        stat_rows = STATS * parts + -STATS * parts % 8
        merged_block, partial = pl.pallas_call(
            functools.partial(merge_kernel, shards, capacity, r, places),
            out_shape=[
                block,
                jax.ShapeDtypeStruct((parts * rows_request // 2 + stat_rows, head_dim), jnp.int32),
            ],
            in_specs=[vmem] * (3 + shards + parts - 1),
            out_specs=[vmem, vmem],
            input_output_aliases={0: 0},
            compiler_params=params,
            name="merge",
        )(staged[r], query_rows, kept_counts, *[messages[i] for i in mine], *partials[: parts - 1])
        merged.append(merged_block)
        partials.append(partial)
    partial = partials[-1]
    partials = [partial] + [shifted(partial, k) for k in range(shards - 1, 0, -1)][::-1]

    merged = pl.pallas_call(
        store_kernel,
        out_shape=pltpu.HBM((pairs, kept_dev, width), jnp.bfloat16),
        in_specs=[vmem] * req_local,
        out_specs=anywhere,
        scratch_shapes=[pltpu.SemaphoreType.DMA((req_local,))],
        compiler_params=params,
        name="unstage",
    )(*merged)

    attended = pl.pallas_call(
        functools.partial(combine_kernel, shards, head_local, kept_dev),
        out_shape=jax.ShapeDtypeStruct(queries.shape, jnp.bfloat16),
        in_specs=[vmem] * (shards + 3),
        out_specs=vmem,
        scratch_shapes=[pltpu.VMEM((shards,) + partial.shape, jnp.int32)],
        compiler_params=params,
        name="combine",
    )(*partials, fresh_top, fresh_total, fresh)
    return (merged.reshape(cache.shape), attended)


def solution(mesh):
    return jax.shard_map(
        body,
        mesh=mesh,
        in_specs=(
            P(("grp", "req"), "hd", "seq", None),
            P(("grp", "req"), "hd", "seq", None),
            P(("grp", "req"), "hd", "seq"),
            P(("grp", "req"), "hd", "seq"),
            P(("grp", "req"), "seq"),
            P(None, ("grp", "req"), "hd", None),
            P(None, ("grp", "req"), "hd", None),
        ),
        out_specs=(P(("grp", "req"), "hd", "seq", None), P(None, ("grp", "req"), "hd", None)),
        check_vma=False,
    )
```

time: 31.4 us -> 30.3 us (0.965)
  waiting for transfers between devices: 8.25 us -> 4.98 us
  starting transfers between devices: 12.9 us -> 14.6 us
  local copies, waits for them, and re-layouts: 1.12 us -> 1.83 us
    ppermute x6 -> x8, waiting for transfers between devices: 8.25 us -> 4.98 us  [shifted(): lax.ppermute(array, 'seq', [(i, (i + k) % shards) for i in range(shards)])]
    ppermute x6 -> x8, starting transfers between devices: 12.9 us -> 14.6 us  [shifted(): lax.ppermute(array, 'seq', [(i, (i + k) % shards) for i in range(shards)])]
    transpose x1, local copies, waits for them, and re-layouts: 0.01 us -> 0.73 us  [body(): fresh_rows = new_rows.transpose(1, 2, 0, 3).reshape(pairs, steps, width)]
    pallas_call x4 -> x5, Pallas kernels: 6.59 us -> 6.44 us  [the longest x2 2.48 us: body(): pl.pallas_call(functools.partial(merge_kernel, shards, capacity, r, place...]
  transfers between devices with their start and end apart: 6 -> 8, of which waited for: 4 -> 4; matrix products, arithmetic and copies ran while one was open for 5% -> 7% of each run, Pallas kernels for 8% -> 13%
where the time goes in v3:
time: 30.3 us; the launch traced here: 30.1 us
  starting transfers between devices  14.6 us (48%)
  Pallas kernels  7.58 us (25%)
  waiting for transfers between devices  4.98 us (16%)
  local copies, waits for them, and re-layouts  1.83 us (6%)
  between operations  0.7 us (2%)
  matrix products  0.37 us (1%)
    ppermute x8, starting transfers between devices, shifted(): lax.ppermute(array, 'seq', [(i, (i + k) % shards) for i in range(shards)])  14.6 us
    ppermute x8, waiting for transfers between devices, shifted(): lax.ppermute(array, 'seq', [(i, (i + k) % shards) for i in range(shards)])  4.98 us
    pallas_call x2, Pallas kernels, body(): pl.pallas_call(functools.partial(merge_kernel, shards, capacity, r, place...  2.48 us
    pallas_call x1, Pallas kernels, body(): pl.pallas_call(functools.partial(pack_kernel, shards, capacity, kept_dev,...  1.41 us
    pallas_call x1, Pallas kernels, body(): pl.pallas_call(load_kernel, out_shape=[block] * req_local, in_specs=[anyw...  1.4 us
    pallas_call x1, Pallas kernels, body(): pl.pallas_call(store_kernel, out_shape=pltpu.HBM((pairs, kept_dev, width)...  1.15 us
    pallas_call x1, Pallas kernels, body(): pl.pallas_call(functools.partial(combine_kernel, shards, head_local, kept...  1.14 us
    reshape x1, local copies, waits for them, and re-layouts, body(): query_rows = queries.reshape(steps, req_local, head_local, group, head_dim)  0.85 us
  transfers between devices with their start and end apart: 8, of which 4 were waited for; matrix products, arithmetic and copies ran while one was open for 7% of the time, Pallas kernels for 13%

profile of v3, /device:TPU:0, one launch (start us, length us, event | category | flops | bytes accessed | tf_op | source)
XLA Modules:
  0.0 30.1 jit_solution(18256007430771237809)
XLA Ops:
  0.6 1.4 %pack.1 = (bf16[272,256]{1,0:T(8,128)(2,1)S(1)}, bf16[272,256]{1,0:T(8,128)(2,1)S(1)}, bf16[136,256]{1,0:T(8,128)(2,1)S(1)}, bf16[136,256]{1,0:T(8,128)(2,1)S(1)...) custom-call(bf16[8,64,256]{2,1,0:T(8,128)(2,1)} %bitcast.19, bf16[8,64]{1,0:T(8,128)(2,1)} %bitcast.25, ...), custom_call_target="tpu_custom_call" | custom-call | tf_op jit(solution)/shard_map/pack/pallas_call | solution.py:289
  2.1 3.1 %collective-permute-start = (bf16[272,256]{1,0:T(8,128)(2,1)S(1)}, bf16[272,256]{1,0:T(8,128)(2,1)S(1)}, u32[]{:S(2)}, u32[]{:S(2)}) collective-permute-start(bf16[272,256]{1,0:T(8,128)(2,1)S(1)} %get-tuple-element.16), channel_id=1, source_target_pairs={{0,4},{4,8},{8,12},{12,0},{1,5},{5,9},{9,13},{13,1},{2,6},{6,10},{... | collective-permute-start | bytes 417800 | tf_op jit(solution)/shard_map/ppermute | solution.py:314
  5.1 2.6 %collective-permute-start.1 = (bf16[136,256]{1,0:T(8,128)(2,1)S(1)}, bf16[136,256]{1,0:T(8,128)(2,1)S(1)}, u32[]{:S(2)}, u32[]{:S(2)}) collective-permute-start(bf16[136,256]{1,0:T(8,128)(2,1)S(1)} %get-tuple-element.17), channel_id=1, source_target_pairs={{0,8},{4,12},{8,0},{12,4},{1,9},{5,13},{9,1},{13,5},{2,10},{6,14},... | collective-permute-start | bytes 208904 | tf_op jit(solution)/shard_map/ppermute | solution.py:314
  7.7 1.3 %collective-permute-start.2 = (bf16[136,256]{1,0:T(8,128)(2,1)S(1)}, bf16[136,256]{1,0:T(8,128)(2,1)S(1)}, u32[]{:S(2)}, u32[]{:S(2)}) collective-permute-start(bf16[136,256]{1,0:T(8,128)(2,1)S(1)} %get-tuple-element.18), channel_id=1, source_target_pairs={{0,12},{4,0},{8,4},{12,8},{1,13},{5,1},{9,5},{13,9},{2,14},{6,2},{... | collective-permute-start | bytes 208904 | tf_op jit(solution)/shard_map/ppermute | solution.py:314
  9.1 0.2 collective-permute-start.3
  9.3 2.8 %collective-permute-start.4 = (bf16[136,256]{1,0:T(8,128)(2,1)S(1)}, bf16[136,256]{1,0:T(8,128)(2,1)S(1)}, u32[]{:S(2)}, u32[]{:S(2)}) collective-permute-start(bf16[136,256]{1,0:T(8,128)(2,1)S(1)} %get-tuple-element.22), channel_id=1, source_target_pairs={{0,12},{4,0},{8,4},{12,8},{1,13},{5,1},{9,5},{13,9},{2,14},{6,2},{... | collective-permute-start | bytes 208904 | tf_op jit(solution)/shard_map/ppermute | solution.py:314
  12.1 0.9 %copy.11 = bf16[4,2,4,8,128]{4,3,0,2,1:T(8,128)(2,1)S(1)} copy(bf16[4,2,4,8,128]{4,3,2,1,0:T(8,128)(2,1)} %bitcast.20) | data formatting | bytes 131072 | tf_op jit(solution)/shard_map/reshape | solution.py:318
  13.0 0.7 %copy.14 = bf16[2,4,4,256]{3,2,1,0:T(4,128)(2,1)S(1)} copy(bf16[2,4,4,256]{3,1,0,2:T(4,128)(2,1)} %bitcast.23) | data formatting | bytes 32768 | tf_op jit(solution)/shard_map/transpose | solution.py:320
  13.7 0.2 fusion.8
  13.9 0.2 fusion.3
  14.1 0.1 reshape.78.refs_4_
  14.2 1.4 %stage.1 = (bf16[4,384,256]{2,1,0:T(8,128)(2,1)S(1)}, bf16[4,384,256]{2,1,0:T(8,128)(2,1)S(1)}) custom-call(bf16[8,384,256]{2,1,0:T(8,128)(2,1)} %bitcast.17), custom_call_target="tpu_custom_call" | custom-call | tf_op jit(solution)/shard_map/stage/pallas_call | solution.py:327
  15.6 0.1 copy.12.refs_2_
  15.7 1.2 %merge.2 = (bf16[4,384,256]{2,1,0:T(8,128)(2,1)S(1)}, s32[72,128]{1,0:T(8,128)S(1)}) custom-call(bf16[4,384,256]{2,1,0:T(8,128)(2,1)S(1)} %get-tuple-element.14.refs_0_, bf16[8,32,128]{2,1,0:T(8,128)(2,1)S(1)} %bitcast.14, s32[2,1]{1,0:T(2,128)S(1)} %copy.12.refs_2_, ...), custom_call_target="tpu_custom_call", output_to_operand_aliasing={{0}: (0, {})} | custom-call | tf_op jit(solution)/shard_map/merge/pallas_call | solution.py:344
  16.9 1.5 %collective-permute-done.3.refs_5_ = bf16[136,256]{1,0:T(8,128)(2,1)S(1)} collective-permute-done((bf16[136,256]{1,0:T(8,128)(2,1)S(1)}, bf16[136,256]{1,0:T(8,128)(2,1)S(1)}, u32[]{:S(2)}, u32[]{:S(2)}) %collective-permute-start.3) | collective-permute-done | bytes 69664 | tf_op jit(solution)/shard_map/ppermute | solution.py:314
  18.4 1.2 %merge.3 = (bf16[4,384,256]{2,1,0:T(8,128)(2,1)S(1)}, s32[136,128]{1,0:T(8,128)S(1)}) custom-call(bf16[4,384,256]{2,1,0:T(8,128)(2,1)S(1)} %get-tuple-element.20.refs_0_, bf16[8,32,128]{2,1,0:T(8,128)(2,1)S(1)} %bitcast.15, s32[2,1]{1,0:T(2,128)S(1)} %copy.12.refs_2_, ...), custom_call_target="tpu_custom_call", output_to_operand_aliasing={{0}: (0, {})} | custom-call | tf_op jit(solution)/shard_map/merge/pallas_call | solution.py:344
  19.6 2.0 %collective-permute-start.5 = (s32[136,128]{1,0:T(8,128)S(1)}, s32[136,128]{1,0:T(8,128)S(1)}, u32[]{:S(2)}, u32[]{:S(2)}) collective-permute-start(s32[136,128]{1,0:T(8,128)S(1)} %get-tuple-element.25.refs_0_), channel_id=1, source_target_pairs={{0,4},{4,8},{8,12},{12,0},{1,5},{5,9},{9,13},{13,1},{2,6},{6,10},{... | collective-permute-start | bytes 208904 | tf_op jit(solution)/shard_map/ppermute | solution.py:314
  21.6 2.1 %collective-permute-start.6 = (s32[136,128]{1,0:T(8,128)S(1)}, s32[136,128]{1,0:T(8,128)S(1)}, u32[]{:S(2)}, u32[]{:S(2)}) collective-permute-start(s32[136,128]{1,0:T(8,128)S(1)} %get-tuple-element.25.refs_0_), channel_id=1, source_target_pairs={{0,8},{4,12},{8,0},{12,4},{1,9},{5,13},{9,1},{13,5},{2,10},{6,14},... | collective-permute-start | bytes 208904 | tf_op jit(solution)/shard_map/ppermute | solution.py:314
  23.8 0.4 %collective-permute-start.7 = (s32[136,128]{1,0:T(8,128)S(1)}, s32[136,128]{1,0:T(8,128)S(1)}, u32[]{:S(2)}, u32[]{:S(2)}) collective-permute-start(s32[136,128]{1,0:T(8,128)S(1)} %get-tuple-element.25.refs_0_), channel_id=1, source_target_pairs={{0,12},{4,0},{8,4},{12,8},{1,13},{5,1},{9,5},{13,9},{2,14},{6,2},{... | collective-permute-start | bytes 208904 | tf_op jit(solution)/shard_map/ppermute | solution.py:314
  24.2 1.2 %unstage.1 = bf16[8,384,256]{2,1,0:T(8,128)(2,1)} custom-call(bf16[4,384,256]{2,1,0:T(8,128)(2,1)S(1)} %get-tuple-element.19.refs_0_, bf16[4,384,256]{2,1,0:T(8,128)(2,1)S(1)} %get-tuple-element.24.refs_1_), custom_call_target="tpu_custom_call" | custom-call | tf_op jit(solution)/shard_map/unstage/pallas_call | solution.py:361
  25.4 1.0 %collective-permute-done.5.refs_1_ = s32[136,128]{1,0:T(8,128)S(1)} collective-permute-done((s32[136,128]{1,0:T(8,128)S(1)}, s32[136,128]{1,0:T(8,128)S(1)}, u32[]{:S(2)}, u32[]{:S(2)}) %collective-permute-start.5) | collective-permute-done | bytes 69664 | tf_op jit(solution)/shard_map/ppermute | solution.py:314
  26.4 2.2 %collective-permute-done.6.refs_2_ = s32[136,128]{1,0:T(8,128)S(1)} collective-permute-done((s32[136,128]{1,0:T(8,128)S(1)}, s32[136,128]{1,0:T(8,128)S(1)}, u32[]{:S(2)}, u32[]{:S(2)}) %collective-permute-start.6) | collective-permute-done | bytes 69664 | tf_op jit(solution)/shard_map/ppermute | solution.py:314
  28.6 0.4 %collective-permute-done.7.refs_3_ = s32[136,128]{1,0:T(8,128)S(1)} collective-permute-done((s32[136,128]{1,0:T(8,128)S(1)}, s32[136,128]{1,0:T(8,128)S(1)}, u32[]{:S(2)}, u32[]{:S(2)}) %collective-permute-start.7) | collective-permute-done | bytes 69664 | tf_op jit(solution)/shard_map/ppermute | solution.py:314
  28.9 1.1 %combine.1 = bf16[4,2,32,128]{3,2,1,0:T(8,128)(2,1)} custom-call(s32[136,128]{1,0:T(8,128)S(1)} %get-tuple-element.25.refs_0_, s32[136,128]{1,0:T(8,128)S(1)} %collective-permute-done.5.refs_1_, s32[136,128]{1,0:T(8,128)S(1)} %collective-permute-done.6.refs_2_, s32[136,128]{1,0:T(8,128)S(1)} %collective-permute-done.7.refs_3_, ...), custom_call_target="tpu_custom_call" | custom-call | tf_op jit(solution)/shard_map/combine/pallas_call | solution.py:371
  (10 shorter events, 0.1 us)
Async XLA Ops:
  0.6 14.9 %copy-start = (s32[2,1]{0,1:T(1,128)S(1)}, s32[2,1]{0,1:T(1,128)}, u32[]{:S(2)}) copy-start(s32[2,1]{0,1:T(1,128)} %param.11) | copy-start | bytes 28
  2.1 13.6 %collective-permute-start = (bf16[272,256]{1,0:T(8,128)(2,1)S(1)}, bf16[272,256]{1,0:T(8,128)(2,1)S(1)}, u32[]{:S(2)}, u32[]{:S(2)}) collective-permute-start(bf16[272,256]{1,0:T(8,128)(2,1)S(1)} %get-tuple-element.16), channel_id=1, source_target_pairs={{0,4},{4,8},{8,12},{12,0},{1,5},{5,9},{9,13},{13,1},{2,6},{6,10},{... | collective-permute-start | bytes 417800 | tf_op jit(solution)/shard_map/ppermute | solution.py:314
  5.1 10.5 %collective-permute-start.1 = (bf16[136,256]{1,0:T(8,128)(2,1)S(1)}, bf16[136,256]{1,0:T(8,128)(2,1)S(1)}, u32[]{:S(2)}, u32[]{:S(2)}) collective-permute-start(bf16[136,256]{1,0:T(8,128)(2,1)S(1)} %get-tuple-element.17), channel_id=1, source_target_pairs={{0,8},{4,12},{8,0},{12,4},{1,9},{5,13},{9,1},{13,5},{2,10},{6,14},... | collective-permute-start | bytes 208904 | tf_op jit(solution)/shard_map/ppermute | solution.py:314
  7.7 8.0 %collective-permute-start.2 = (bf16[136,256]{1,0:T(8,128)(2,1)S(1)}, bf16[136,256]{1,0:T(8,128)(2,1)S(1)}, u32[]{:S(2)}, u32[]{:S(2)}) collective-permute-start(bf16[136,256]{1,0:T(8,128)(2,1)S(1)} %get-tuple-element.18), channel_id=1, source_target_pairs={{0,12},{4,0},{8,4},{12,8},{1,13},{5,1},{9,5},{13,9},{2,14},{6,2},{... | collective-permute-start | bytes 208904 | tf_op jit(solution)/shard_map/ppermute | solution.py:314
  9.1 9.3 %collective-permute-start.3 = (bf16[136,256]{1,0:T(8,128)(2,1)S(1)}, bf16[136,256]{1,0:T(8,128)(2,1)S(1)}, u32[]{:S(2)}, u32[]{:S(2)}) collective-permute-start(bf16[136,256]{1,0:T(8,128)(2,1)S(1)} %get-tuple-element.21), channel_id=1, source_target_pairs={{0,8},{4,12},{8,0},{12,4},{1,9},{5,13},{9,1},{13,5},{2,10},{6,14},... | collective-permute-start | bytes 208904 | tf_op jit(solution)/shard_map/ppermute | solution.py:314
  9.3 9.1 %collective-permute-start.4 = (bf16[136,256]{1,0:T(8,128)(2,1)S(1)}, bf16[136,256]{1,0:T(8,128)(2,1)S(1)}, u32[]{:S(2)}, u32[]{:S(2)}) collective-permute-start(bf16[136,256]{1,0:T(8,128)(2,1)S(1)} %get-tuple-element.22), channel_id=1, source_target_pairs={{0,12},{4,0},{8,4},{12,8},{1,13},{5,1},{9,5},{13,9},{2,14},{6,2},{... | collective-permute-start | bytes 208904 | tf_op jit(solution)/shard_map/ppermute | solution.py:314
  19.6 6.8 %collective-permute-start.5 = (s32[136,128]{1,0:T(8,128)S(1)}, s32[136,128]{1,0:T(8,128)S(1)}, u32[]{:S(2)}, u32[]{:S(2)}) collective-permute-start(s32[136,128]{1,0:T(8,128)S(1)} %get-tuple-element.25.refs_0_), channel_id=1, source_target_pairs={{0,4},{4,8},{8,12},{12,0},{1,5},{5,9},{9,13},{13,1},{2,6},{6,10},{... | collective-permute-start | bytes 208904 | tf_op jit(solution)/shard_map/ppermute | solution.py:314
  21.6 6.9 %collective-permute-start.6 = (s32[136,128]{1,0:T(8,128)S(1)}, s32[136,128]{1,0:T(8,128)S(1)}, u32[]{:S(2)}, u32[]{:S(2)}) collective-permute-start(s32[136,128]{1,0:T(8,128)S(1)} %get-tuple-element.25.refs_0_), channel_id=1, source_target_pairs={{0,8},{4,12},{8,0},{12,4},{1,9},{5,13},{9,1},{13,5},{2,10},{6,14},... | collective-permute-start | bytes 208904 | tf_op jit(solution)/shard_map/ppermute | solution.py:314
  23.8 5.2 %collective-permute-start.7 = (s32[136,128]{1,0:T(8,128)S(1)}, s32[136,128]{1,0:T(8,128)S(1)}, u32[]{:S(2)}, u32[]{:S(2)}) collective-permute-start(s32[136,128]{1,0:T(8,128)S(1)} %get-tuple-element.25.refs_0_), channel_id=1, source_target_pairs={{0,12},{4,0},{8,4},{12,8},{1,13},{5,1},{9,5},{13,9},{2,14},{6,2},{... | collective-permute-start | bytes 208904 | tf_op jit(solution)/shard_map/ppermute | solution.py:314

commit v4 on v3

v4 whole, which is shorter than its diff:
```python
import functools
import math

import jax
import jax.numpy as jnp
from jax import lax
from jax.experimental import pallas as pl
from jax.experimental.pallas import tpu as pltpu
from jax.sharding import PartitionSpec as P

STATS = 4
CODE_MAX = 32767.0
LEVELS = 16.0
SMALLEST = 1e-36
FRACTION = 2.0**30
VMEM_BYTES = 8 * 1024 * 1024


def dot(a, b, contract):
    return lax.dot_general(a, b, (contract, ((), ())), preferred_element_type=jnp.float32)


def apart(holder, me, shards):
    if shards & (shards - 1):
        return jnp.where(holder >= me, holder - me, holder - me + shards)
    return jnp.bitwise_xor(holder, me)


def at_distance(i, k, shards):
    return (i + k) % shards if shards & (shards - 1) else i ^ k


def pack_kernel(shards, capacity, kept_dev, requests, plan, *refs):
    message_refs = refs[3 : 3 + len(plan)]
    evicted_ref, weight_ref, target_ref, sems = refs[3 + len(plan) :]
    loads = [
        pltpu.make_async_copy(refs[i], refs[3 + len(plan) + i], sems.at[i]) for i in (2, 1, 0)
    ]
    for load in loads:
        load.start()
    pairs, evict_dev, width = evicted_ref.shape
    slots = shards * capacity
    me = lax.axis_index("seq")
    loads[0].wait()
    loads[1].wait()
    targets = target_ref[...]
    holder = jnp.zeros_like(targets)
    for block in range(1, shards):
        holder += (targets >= block * kept_dev).astype(jnp.int32)
    centred = targets - holder * kept_dev - kept_dev // 2
    distance = apart(holder, me, shards)
    owned = jnp.concatenate(
        [(distance == k).astype(jnp.float32) for k in range(shards)], axis=0
    )
    before = lax.broadcasted_iota(jnp.int32, (evict_dev, evict_dev), 0) < lax.broadcasted_iota(
        jnp.int32, (evict_dev, evict_dev), 1
    )
    prefix = dot(owned.astype(jnp.bfloat16), before.astype(jnp.bfloat16), ((1,), (0,)))
    ranked = owned * prefix
    rank = ranked[0:pairs]
    for k in range(1, shards):
        rank += ranked[k * pairs : (k + 1) * pairs]
    slot = distance * capacity + rank.astype(jnp.int32)
    facts = jnp.concatenate(
        [weight_ref[...].astype(jnp.float32), centred.astype(jnp.float32)], axis=0
    ).astype(jnp.bfloat16)
    slot_index = lax.broadcasted_iota(jnp.int32, (slots, evict_dev), 0)
    pair_index = lax.broadcasted_iota(jnp.int32, (pairs, slots), 0)
    weights = jnp.zeros((pairs, slots), jnp.float32)
    positions = jnp.zeros((pairs, slots), jnp.float32)
    rows = []
    loads[2].wait()
    for p in range(pairs):
        placing = (slot_index == slot[p : p + 1, :]).astype(jnp.float32).astype(jnp.bfloat16)
        rows.append(dot(placing, evicted_ref[p], ((1,), (0,))))
        placed = dot(facts, placing, ((1,), (1,)))
        weights = jnp.where(pair_index == p, placed[0:pairs], weights)
        positions = jnp.where(pair_index == p, placed[pairs:], positions)
    meta = jnp.concatenate([weights, positions], axis=1)
    heads = pairs // requests
    for message_ref, (k, members) in zip(message_refs, plan):
        message = [
            rows[r * heads + h][k * capacity : (k + 1) * capacity]
            for r in members
            for h in range(heads)
        ]
        message_ref[...] = jnp.concatenate(message + [meta], axis=0).astype(jnp.bfloat16)


def load_kernel(from_ref, *refs):
    to_refs, sems = refs[:-1], refs[-1]
    each = to_refs[0].shape[0]
    copies = [
        pltpu.make_async_copy(from_ref.at[pl.ds(r * each, each)], to_ref, sems.at[r])
        for r, to_ref in enumerate(to_refs)
    ]
    for copy in copies:
        copy.start()
    for copy in copies:
        copy.wait()


def store_kernel(*refs):
    from_refs, to_ref, sems = refs[:-2], refs[-2], refs[-1]
    each = from_refs[0].shape[0]
    copies = [
        pltpu.make_async_copy(from_ref, to_ref.at[pl.ds(r * each, each)], sems.at[r])
        for r, from_ref in enumerate(from_refs)
    ]
    for copy in copies:
        copy.start()
    for copy in copies:
        copy.wait()


def merge_kernel(shards, capacity, requests, request, parts, *refs):
    cache_ref, query_ref, count_ref = refs[:3]
    message_refs = refs[3 : 3 + shards]
    before_refs = refs[3 + shards : 3 + shards + 2 * request]
    merged_ref, *out_refs = refs[3 + shards + 2 * request :]
    heads, kept_dev, width = merged_ref.shape
    pairs = requests * heads
    head_dim = width // 2
    rows_each = query_ref.shape[1]
    rows_request = heads * rows_each
    slots = shards * capacity
    scale = 1.0 / math.sqrt(head_dim)
    order = sorted(range(shards), key=lambda i: parts[i][0])
    firsts = [members.index(request) * heads * capacity for _, members in parts]
    lane = lax.broadcasted_iota(jnp.int32, (pairs, slots), 1)
    weights = jnp.zeros((pairs, slots), jnp.float32)
    positions = jnp.zeros((pairs, slots), jnp.float32)
    received = []
    for (k, members), message_ref in zip(parts, message_refs):
        meta = message_ref[len(members) * heads * capacity :, :].astype(jnp.float32)
        mine = jnp.logical_and(lane >= k * capacity, lane < (k + 1) * capacity)
        weights = jnp.where(mine, meta[:, 0:slots], weights)
        positions = jnp.where(mine, meta[:, slots : 2 * slots], positions)
        if capacity % 16:
            received.append(message_ref[...].astype(jnp.float32))
    positions, weights = positions.astype(jnp.bfloat16), weights.astype(jnp.bfloat16)
    kept_index = lax.broadcasted_iota(jnp.int32, (kept_dev, slots), 0) - kept_dev // 2
    kept_index = kept_index.astype(jnp.float32).astype(jnp.bfloat16)
    nothing = jnp.zeros((), jnp.bfloat16)
    together = 2 - heads % 2
    twin_row = lax.broadcasted_iota(jnp.int32, (together * slots, together * head_dim), 0) // slots
    twin_lane = lax.broadcasted_iota(jnp.int32, twin_row.shape, 1) // head_dim
    twin = (twin_row == twin_lane).astype(jnp.float32).astype(jnp.bfloat16)
    for first in range(0, heads, together):
        placings = []
        for h in range(first, first + together):
            p = request * heads + h
            placings.append(
                jnp.where(kept_index == positions[p : p + 1, :], weights[p : p + 1, :], nothing)
            )
        share = 1.0 / (1.0 + dot(jnp.concatenate(placings, axis=1), twin, ((1,), (0,))))
        for i, h in enumerate(range(first, first + together)):
            if capacity % 16:
                rows = [received[j][firsts[j] + h * capacity :][:capacity] for j in order]
                rows = jnp.concatenate(rows, axis=0).astype(jnp.bfloat16)
            else:
                rows = [
                    message_refs[j][pl.ds(firsts[j] + h * capacity, capacity), :] for j in order
                ]
                rows = jnp.concatenate(rows, axis=0)
            stored = cache_ref[h].astype(jnp.float32) + dot(placings[i], rows, ((1,), (0,)))
            own = share[:, i * head_dim : (i + 1) * head_dim]
            merged_ref[h, :, 0:head_dim] = (stored[:, 0:head_dim] * own).astype(jnp.bfloat16)
            merged_ref[h, :, head_dim:] = (stored[:, head_dim:] * own).astype(jnp.bfloat16)
    scores = [
        dot(query_ref[request * heads + h], merged_ref[h, :, 0:head_dim], ((1,), (1,)))
        for h in range(heads)
    ]
    scores = jnp.concatenate(scores, axis=0) * scale
    column = lax.broadcasted_iota(jnp.int32, scores.shape, 1)
    scores = jnp.where(column < count_ref[request : request + 1, :], scores, -1e30)
    top = jnp.max(scores, axis=1, keepdims=True)
    exponent = jnp.exp(scores - top)
    total = jnp.sum(exponent, axis=1, keepdims=True)
    exponent = exponent.astype(jnp.bfloat16)
    weighted = [
        dot(
            exponent[h * rows_each : (h + 1) * rows_each],
            merged_ref[h, :, head_dim:],
            ((1,), (0,)),
        )
        for h in range(heads)
    ]
    weighted = jnp.concatenate(weighted, axis=0)
    largest = jnp.max(jnp.abs(weighted), axis=1, keepdims=True)
    level = jnp.ceil(jnp.log2(jnp.maximum(largest, SMALLEST)) * LEVELS)
    codes = jnp.floor(weighted * (CODE_MAX / jnp.exp2(level / LEVELS)) + 0.5)
    codes = jnp.clip(codes, -CODE_MAX, CODE_MAX).astype(jnp.int32)
    stat_lane = lax.broadcasted_iota(jnp.int32, weighted.shape, 1)
    stats = jnp.zeros(weighted.shape, jnp.float32)
    for i, stat in enumerate((top, total, level)):
        stats = jnp.where(stat_lane == i * requests + request, stat, stats)
    if request < requests - 1:
        out_refs[0][...] = codes
        out_refs[1][...] = stats
        return
    (partial_ref,) = out_refs
    codes = [before_refs[2 * r][...] for r in range(request)] + [codes]
    codes = jnp.concatenate(codes, axis=0)
    for r in range(request):
        stats += before_refs[2 * r + 1][...]
    half = requests * rows_request // 2
    partial_ref[0:half, :] = (codes[0:half] << 16) | (codes[half:] & 0xFFFF)
    stats = jnp.transpose(stats)
    top, total, level = (stats[i * requests : (i + 1) * requests] for i in range(3))
    whole = jnp.floor(top)
    stats = [
        whole.astype(jnp.int32),
        ((top - whole) * FRACTION).astype(jnp.int32),
        (total * (FRACTION / kept_dev)).astype(jnp.int32),
        level.astype(jnp.int32),
    ]
    filler = -STATS * requests % 8
    if filler:
        stats.append(jnp.zeros((filler, rows_request), jnp.int32))
    partial_ref[half:, :] = jnp.concatenate(stats, axis=0)


def combine_kernel(shards, heads, kept_dev, distances, *refs):
    partial_refs = refs[:shards]
    fresh_top_ref, fresh_total_ref, fresh_ref, out_ref, ordered = refs[shards:]
    steps, requests, query_local, head_dim = out_ref.shape
    group = query_local // heads
    rows_each = steps * group
    rows_request = heads * rows_each
    half = requests * rows_request // 2
    me = lax.axis_index("seq")
    for k, partial_ref in zip(distances, partial_refs):
        source = jnp.where(me >= k, me - k, me - k + shards)
        ordered[source] = partial_ref[...]
    tops, totals, units = [fresh_top_ref[...]], [fresh_total_ref[...]], [1.0]
    for b in range(shards):
        stats = ordered[b, half : half + STATS * requests, :].astype(jnp.float32)
        whole, rest, total, level = (
            stats[i * requests : (i + 1) * requests] for i in range(STATS)
        )
        tops.append(whole + rest * (1.0 / FRACTION))
        totals.append(total * (kept_dev / FRACTION))
        units.append(jnp.exp2(level / LEVELS) * (1.0 / CODE_MAX))
    highest = functools.reduce(jnp.maximum, tops)
    scales = [jnp.exp(top - highest) for top in tops]
    share = 1.0 / sum(a * b for a, b in zip(totals, scales))
    factors = [s * u * share for s, u in zip(scales, units)]
    padding = -len(factors) * requests % 8
    if padding:
        factors.append(jnp.zeros((padding, rows_request), jnp.float32))
    factors = jnp.transpose(jnp.concatenate(factors, axis=0))
    for r in range(requests):
        first = r * rows_request
        result = fresh_ref[first : first + rows_request, :] * factors[:, r : r + 1]
        low = first % half
        for b in range(shards):
            words = ordered[b, low : low + rows_request, :]
            codes = words >> 16 if first < half else (words << 16) >> 16
            column = (b + 1) * requests + r
            result += codes.astype(jnp.float32) * factors[:, column : column + 1]
        for s in range(steps):
            pieces = [
                result[h * rows_each + s * group : h * rows_each + (s + 1) * group]
                for h in range(heads)
            ]
            out_ref[s, r] = jnp.concatenate(pieces, axis=0).astype(jnp.bfloat16)


def fresh_block(query_rows, fresh_rows, group):
    head_dim = query_rows.shape[-1]
    scores = jnp.einsum(
        "pqd,pjd->pqj", query_rows, fresh_rows[..., :head_dim], preferred_element_type=jnp.float32
    ) * (1.0 / math.sqrt(head_dim))
    step_index = jnp.arange(query_rows.shape[1], dtype=jnp.int32) // group
    allowed = jnp.arange(fresh_rows.shape[1], dtype=jnp.int32)[None, :] <= step_index[:, None]
    scores = jnp.where(allowed[None], scores, -1e30)
    top = jnp.max(scores, axis=-1)
    exponent = jnp.exp(scores - top[..., None])
    weighted = jnp.einsum(
        "pqj,pjd->pqd",
        exponent.astype(jnp.bfloat16),
        fresh_rows[..., head_dim:],
        preferred_element_type=jnp.float32,
    )
    return (top, jnp.sum(exponent, axis=-1), weighted)


def body(cache, evicted, merge_weight, targets, kept_counts, queries, new_rows):
    req_local, head_local, kept_dev, width = cache.shape
    head_dim = width // 2
    shards = lax.axis_size("seq")
    evict_dev = evicted.shape[2]
    capacity = max(2, 2 * evict_dev // shards)
    pairs = req_local * head_local
    steps, _, query_local, _ = queries.shape
    group = query_local // head_local
    rows_each = steps * group
    vmem = pl.BlockSpec(memory_space=pltpu.VMEM)
    anywhere = pl.BlockSpec(memory_space=pl.ANY)

    def in_hbm(array):
        return pltpu.with_memory_space_constraint(array, pltpu.HBM)

    params = pltpu.CompilerParams(vmem_limit_bytes=VMEM_BYTES)

    rows_request = head_local * rows_each
    distances = [0] + sorted(range(1, shards), key=lambda k: (k & (k - 1), -k))
    every = tuple(range(req_local))
    plan = [(k, every) for k in distances[:-1]] + [(distances[-1], (r,)) for r in every]
    packed = pl.pallas_call(
        functools.partial(pack_kernel, shards, capacity, kept_dev, req_local, plan),
        out_shape=[
            jax.ShapeDtypeStruct((len(m) * head_local * capacity + pairs, width), jnp.bfloat16)
            for _, m in plan
        ],
        in_specs=[anywhere] * 3,
        out_specs=[vmem] * len(plan),
        scratch_shapes=[
            pltpu.VMEM((pairs, evict_dev, width), jnp.bfloat16),
            pltpu.VMEM((pairs, evict_dev), jnp.bfloat16),
            pltpu.VMEM((pairs, evict_dev), jnp.int32),
            pltpu.SemaphoreType.DMA((3,)),
        ],
        compiler_params=params,
        name="pack",
    )(
        in_hbm(evicted.reshape(pairs, evict_dev, width)),
        in_hbm(merge_weight.reshape(pairs, evict_dev)),
        in_hbm(targets.reshape(pairs, evict_dev)),
    )

    messages = [packed[0]]
    for (k, _), message in zip(plan[1:], packed[1:]):
        pairing = [(i, at_distance(i, k, shards)) for i in range(shards)]
        messages.append(lax.ppermute(message, "seq", pairing))

    query_rows = queries.reshape(steps, req_local, head_local, group, head_dim)
    query_rows = query_rows.transpose(1, 2, 0, 3, 4).reshape(pairs, rows_each, head_dim)
    fresh_rows = new_rows.transpose(1, 2, 0, 3).reshape(pairs, steps, width)
    fresh_top, fresh_total, fresh = fresh_block(query_rows, fresh_rows, group)
    fresh_top = fresh_top.reshape(req_local, rows_request)
    fresh_total = fresh_total.reshape(req_local, rows_request)
    fresh = fresh.reshape(pairs * rows_each, head_dim)

    block = jax.ShapeDtypeStruct((head_local, kept_dev, width), jnp.bfloat16)
    staged = pl.pallas_call(
        load_kernel,
        out_shape=[block] * req_local,
        in_specs=[anywhere],
        out_specs=[vmem] * req_local,
        scratch_shapes=[pltpu.SemaphoreType.DMA((req_local,))],
        compiler_params=params,
        name="stage",
    )(in_hbm(cache.reshape(pairs, kept_dev, width)))

    stat_rows = STATS * req_local + -STATS * req_local % 8
    partial_shape = (pairs * rows_each // 2 + stat_rows, head_dim)
    kinds = [((rows_request, head_dim), jnp.int32), ((rows_request, head_dim), jnp.float32)]
    merged, before = [], []
    for r in range(req_local):
        mine = [i for i, (_, m) in enumerate(plan) if r in m]
        if r == req_local - 1:
            kinds = [(partial_shape, jnp.int32)]
        merged_block, *out = pl.pallas_call(
            functools.partial(
                merge_kernel, shards, capacity, req_local, r, [plan[i] for i in mine]
            ),
            out_shape=[block] + [jax.ShapeDtypeStruct(*kind) for kind in kinds],
            in_specs=[vmem] * (3 + shards + len(before)),
            out_specs=[vmem] * (1 + len(kinds)),
            input_output_aliases={0: 0},
            compiler_params=params,
            name="merge",
        )(staged[r], query_rows, kept_counts, *[messages[i] for i in mine], *before)
        merged.append(merged_block)
        before += out
    partial = before[-1]

    shifts = list(range(shards))
    partials = [partial]
    for k in shifts[1:]:
        pairing = [(i, (i + k) % shards) for i in range(shards)]
        partials.append(lax.ppermute(partial, "seq", pairing))

    merged = pl.pallas_call(
        store_kernel,
        out_shape=pltpu.HBM((pairs, kept_dev, width), jnp.bfloat16),
        in_specs=[vmem] * req_local,
        out_specs=anywhere,
        scratch_shapes=[pltpu.SemaphoreType.DMA((req_local,))],
        compiler_params=params,
        name="unstage",
    )(*merged)

    attended = pl.pallas_call(
        functools.partial(combine_kernel, shards, head_local, kept_dev, shifts),
        out_shape=jax.ShapeDtypeStruct(queries.shape, jnp.bfloat16),
        in_specs=[vmem] * (shards + 3),
        out_specs=vmem,
        scratch_shapes=[pltpu.VMEM((shards,) + partial.shape, jnp.int32)],
        compiler_params=params,
        name="combine",
    )(*partials, fresh_top, fresh_total, fresh)
    return (merged.reshape(cache.shape), attended)


def solution(mesh):
    return jax.shard_map(
        body,
        mesh=mesh,
        in_specs=(
            P(("grp", "req"), "hd", "seq", None),
            P(("grp", "req"), "hd", "seq", None),
            P(("grp", "req"), "hd", "seq"),
            P(("grp", "req"), "hd", "seq"),
            P(("grp", "req"), "seq"),
            P(None, ("grp", "req"), "hd", None),
            P(None, ("grp", "req"), "hd", None),
        ),
        out_specs=(P(("grp", "req"), "hd", "seq", None), P(None, ("grp", "req"), "hd", None)),
        check_vma=False,
    )
```

time: 30.3 us -> 29.6 us (0.977)
  waiting for transfers between devices: 4.98 us -> 2.57 us
  starting transfers between devices: 14.6 us -> 16.4 us
    ppermute x8 -> x7, waiting for transfers between devices: 4.98 us -> 2.57 us  [the longest x3 1.59 us: body(): partials.append(lax.ppermute(partial, 'seq', pairing))]
    ppermute x8 -> x7, starting transfers between devices: 14.6 us -> 16.4 us  [the longest x4 9.5 us: body(): messages.append(lax.ppermute(message, 'seq', pairing))]
  transfers between devices with their start and end apart: 8 -> 7, of which waited for: 4 -> 2; matrix products, arithmetic and copies ran while one was open for 7% -> 8% of each run, Pallas kernels for 13% -> 13%
where the time goes in v4:
time: 29.6 us; the launch traced here: 29.4 us
  starting transfers between devices  16.4 us (55%)
  Pallas kernels  7.46 us (25%)
  waiting for transfers between devices  2.57 us (9%)
  local copies, waits for them, and re-layouts  1.83 us (6%)
  between operations  0.71 us (2%)
  matrix products  0.37 us (1%)
    ppermute x4, starting transfers between devices, body(): messages.append(lax.ppermute(message, 'seq', pairing))  9.5 us
    ppermute x3, starting transfers between devices, body(): partials.append(lax.ppermute(partial, 'seq', pairing))  6.9 us
    pallas_call x2, Pallas kernels, body(): pl.pallas_call(functools.partial(merge_kernel, shards, capacity, req_loca...  2.42 us
    ppermute x3, waiting for transfers between devices, body(): partials.append(lax.ppermute(partial, 'seq', pairing))  1.59 us
    pallas_call x1, Pallas kernels, body(): pl.pallas_call(functools.partial(pack_kernel, shards, capacity, kept_dev,...  1.41 us
    pallas_call x1, Pallas kernels, body(): pl.pallas_call(load_kernel, out_shape=[block] * req_local, in_specs=[anyw...  1.4 us
    pallas_call x1, Pallas kernels, body(): pl.pallas_call(store_kernel, out_shape=pltpu.HBM((pairs, kept_dev, width)...  1.15 us
    pallas_call x1, Pallas kernels, body(): pl.pallas_call(functools.partial(combine_kernel, shards, head_local, kept...  1.07 us
  transfers between devices with their start and end apart: 7, of which 2 were waited for; matrix products, arithmetic and copies ran while one was open for 8% of the time, Pallas kernels for 13%

profile of v4, /device:TPU:0, one launch (start us, length us, event | category | flops | bytes accessed | tf_op | source)
XLA Modules:
  0.0 29.4 jit_solution(742885010156743865)
XLA Ops:
  0.6 1.4 %pack.1 = (bf16[264,256]{1,0:T(8,128)(2,1)S(1)}, bf16[264,256]{1,0:T(8,128)(2,1)S(1)}, bf16[264,256]{1,0:T(8,128)(2,1)S(1)}, bf16[136,256]{1,0:T(8,128)(2,1)S(1)}, bf16[136,256]{1,0:T(8,128)(2,1)S(1)}) custom-call(bf16[8,64,256]{2,1,0:T(8,128)(2,1)} %bitcast.19, bf16[8,64]{1,0:T(8,128)(2,1)} %bitcast.25, s32[8,64]{1,0:T(8,128)} %bitcast.24), custom_call_target="tpu_custom_call" | custom-call | tf_op jit(solution)/shard_map/pack/pallas_call | solution.py:311
  2.1 4.1 %collective-permute-start = (bf16[264,256]{1,0:T(8,128)(2,1)S(1)}, bf16[264,256]{1,0:T(8,128)(2,1)S(1)}, u32[]{:S(2)}, u32[]{:S(2)}) collective-permute-start(bf16[264,256]{1,0:T(8,128)(2,1)S(1)} %get-tuple-element.16), channel_id=1, source_target_pairs={{0,8},{4,12},{8,0},{12,4},{1,9},{5,13},{9,1},{13,5},{2,10},{6,14},... | collective-permute-start | bytes 405512 | tf_op jit(solution)/shard_map/ppermute | solution.py:336
  6.2 1.6 %collective-permute-start.1 = (bf16[264,256]{1,0:T(8,128)(2,1)S(1)}, bf16[264,256]{1,0:T(8,128)(2,1)S(1)}, u32[]{:S(2)}, u32[]{:S(2)}) collective-permute-start(bf16[264,256]{1,0:T(8,128)(2,1)S(1)} %get-tuple-element.17), channel_id=1, source_target_pairs={{0,4},{4,0},{8,12},{12,8},{1,5},{5,1},{9,13},{13,9},{2,6},{6,2},{1... | collective-permute-start | bytes 405512 | tf_op jit(solution)/shard_map/ppermute | solution.py:336
  7.7 0.0 collective-permute-start.2
  7.7 3.8 %collective-permute-start.3 = (bf16[136,256]{1,0:T(8,128)(2,1)S(1)}, bf16[136,256]{1,0:T(8,128)(2,1)S(1)}, u32[]{:S(2)}, u32[]{:S(2)}) collective-permute-start(bf16[136,256]{1,0:T(8,128)(2,1)S(1)} %get-tuple-element.21), channel_id=1, source_target_pairs={{0,12},{4,8},{8,4},{12,0},{1,13},{5,9},{9,5},{13,1},{2,14},{6,10},... | collective-permute-start | bytes 208904 | tf_op jit(solution)/shard_map/ppermute | solution.py:336
  11.6 0.9 %copy.11 = bf16[4,2,4,8,128]{4,3,0,2,1:T(8,128)(2,1)S(1)} copy(bf16[4,2,4,8,128]{4,3,2,1,0:T(8,128)(2,1)} %bitcast.20) | data formatting | bytes 131072 | tf_op jit(solution)/shard_map/reshape | solution.py:338
  12.4 0.7 %copy.14 = bf16[2,4,4,256]{3,2,1,0:T(4,128)(2,1)S(1)} copy(bf16[2,4,4,256]{3,1,0,2:T(4,128)(2,1)} %bitcast.23) | data formatting | bytes 32768 | tf_op jit(solution)/shard_map/transpose | solution.py:340
  13.2 0.2 fusion.8
  13.3 0.2 fusion.3
  13.5 0.1 reshape.78.refs_4_
  13.6 1.4 %stage.1 = (bf16[4,384,256]{2,1,0:T(8,128)(2,1)S(1)}, bf16[4,384,256]{2,1,0:T(8,128)(2,1)S(1)}) custom-call(bf16[8,384,256]{2,1,0:T(8,128)(2,1)} %bitcast.17), custom_call_target="tpu_custom_call" | custom-call | tf_op jit(solution)/shard_map/stage/pallas_call | solution.py:347
  15.0 0.1 copy.12.refs_2_
  15.1 1.0 %collective-permute-done.2.refs_6_ = bf16[136,256]{1,0:T(8,128)(2,1)S(1)} collective-permute-done((bf16[136,256]{1,0:T(8,128)(2,1)S(1)}, bf16[136,256]{1,0:T(8,128)(2,1)S(1)}, u32[]{:S(2)}, u32[]{:S(2)}) %collective-permute-start.2) | collective-permute-done | bytes 69664 | tf_op jit(solution)/shard_map/ppermute | solution.py:336
  16.1 0.0 collective-permute-done.refs_4_
  16.1 0.0 collective-permute-done.1.refs_5_
  16.1 1.2 %merge.2 = (bf16[4,384,256]{2,1,0:T(8,128)(2,1)S(1)}, s32[128,128]{1,0:T(8,128)S(1)}, f32[128,128]{1,0:T(8,128)S(1)}) custom-call(bf16[4,384,256]{2,1,0:T(8,128)(2,1)S(1)} %get-tuple-element.14.refs_0_, bf16[8,32,128]{2,1,0:T(8,128)(2,1)S(1)} %bitcast.14, s32[2,1]{1,0:T(2,128)S(1)} %copy.12.refs_2_, ...), custom_call_target="tpu_custom_call", output_to_operand_aliasing={{0}: (0, {})} | custom-call | tf_op jit(solution)/shard_map/merge/pallas_call | solution.py:365
  17.3 1.2 %merge.3 = (bf16[4,384,256]{2,1,0:T(8,128)(2,1)S(1)}, s32[136,128]{1,0:T(8,128)S(1)}) custom-call(bf16[4,384,256]{2,1,0:T(8,128)(2,1)S(1)} %get-tuple-element.20.refs_0_, bf16[8,32,128]{2,1,0:T(8,128)(2,1)S(1)} %bitcast.15, s32[2,1]{1,0:T(2,128)S(1)} %copy.12.refs_2_, ...), custom_call_target="tpu_custom_call", output_to_operand_aliasing={{0}: (0, {})} | custom-call | tf_op jit(solution)/shard_map/merge/pallas_call | solution.py:365
  18.5 2.4 %collective-permute-start.4 = (s32[136,128]{1,0:T(8,128)S(1)}, s32[136,128]{1,0:T(8,128)S(1)}, u32[]{:S(2)}, u32[]{:S(2)}) collective-permute-start(s32[136,128]{1,0:T(8,128)S(1)} %get-tuple-element.25.refs_0_), channel_id=1, source_target_pairs={{0,4},{4,8},{8,12},{12,0},{1,5},{5,9},{9,13},{13,1},{2,6},{6,10},{... | collective-permute-start | bytes 208904 | tf_op jit(solution)/shard_map/ppermute | solution.py:384
  20.9 1.7 %collective-permute-start.5 = (s32[136,128]{1,0:T(8,128)S(1)}, s32[136,128]{1,0:T(8,128)S(1)}, u32[]{:S(2)}, u32[]{:S(2)}) collective-permute-start(s32[136,128]{1,0:T(8,128)S(1)} %get-tuple-element.25.refs_0_), channel_id=1, source_target_pairs={{0,8},{4,12},{8,0},{12,4},{1,9},{5,13},{9,1},{13,5},{2,10},{6,14},... | collective-permute-start | bytes 208904 | tf_op jit(solution)/shard_map/ppermute | solution.py:384
  22.6 2.8 %collective-permute-start.6 = (s32[136,128]{1,0:T(8,128)S(1)}, s32[136,128]{1,0:T(8,128)S(1)}, u32[]{:S(2)}, u32[]{:S(2)}) collective-permute-start(s32[136,128]{1,0:T(8,128)S(1)} %get-tuple-element.25.refs_0_), channel_id=1, source_target_pairs={{0,12},{4,0},{8,4},{12,8},{1,13},{5,1},{9,5},{13,9},{2,14},{6,2},{... | collective-permute-start | bytes 208904 | tf_op jit(solution)/shard_map/ppermute | solution.py:384
  25.5 0.1 reshape.79.refs_5_
  25.5 1.2 %unstage.1 = bf16[8,384,256]{2,1,0:T(8,128)(2,1)} custom-call(bf16[4,384,256]{2,1,0:T(8,128)(2,1)S(1)} %get-tuple-element.19.refs_0_, bf16[4,384,256]{2,1,0:T(8,128)(2,1)S(1)} %get-tuple-element.24.refs_1_), custom_call_target="tpu_custom_call" | custom-call | tf_op jit(solution)/shard_map/unstage/pallas_call | solution.py:386
  26.7 1.6 %collective-permute-done.5.refs_2_ = s32[136,128]{1,0:T(8,128)S(1)} collective-permute-done((s32[136,128]{1,0:T(8,128)S(1)}, s32[136,128]{1,0:T(8,128)S(1)}, u32[]{:S(2)}, u32[]{:S(2)}) %collective-permute-start.5) | collective-permute-done | bytes 69664 | tf_op jit(solution)/shard_map/ppermute | solution.py:384
  28.3 1.1 %combine.1 = bf16[4,2,32,128]{3,2,1,0:T(8,128)(2,1)} custom-call(s32[136,128]{1,0:T(8,128)S(1)} %get-tuple-element.25.refs_0_, s32[136,128]{1,0:T(8,128)S(1)} %collective-permute-done.4.refs_1_, s32[136,128]{1,0:T(8,128)S(1)} %collective-permute-done.5.refs_2_, s32[136,128]{1,0:T(8,128)S(1)} %collective-permute-done.6.refs_3_, ...), custom_call_target="tpu_custom_call" | custom-call | tf_op jit(solution)/shard_map/combine/pallas_call | solution.py:396
  (8 shorter events, 0.0 us)
Async XLA Ops:
  0.6 14.4 %copy-start = (s32[2,1]{0,1:T(1,128)S(1)}, s32[2,1]{0,1:T(1,128)}, u32[]{:S(2)}) copy-start(s32[2,1]{0,1:T(1,128)} %param.11) | copy-start | bytes 28
  2.1 14.0 %collective-permute-start = (bf16[264,256]{1,0:T(8,128)(2,1)S(1)}, bf16[264,256]{1,0:T(8,128)(2,1)S(1)}, u32[]{:S(2)}, u32[]{:S(2)}) collective-permute-start(bf16[264,256]{1,0:T(8,128)(2,1)S(1)} %get-tuple-element.16), channel_id=1, source_target_pairs={{0,8},{4,12},{8,0},{12,4},{1,9},{5,13},{9,1},{13,5},{2,10},{6,14},... | collective-permute-start | bytes 405512 | tf_op jit(solution)/shard_map/ppermute | solution.py:336
  6.2 9.9 %collective-permute-start.1 = (bf16[264,256]{1,0:T(8,128)(2,1)S(1)}, bf16[264,256]{1,0:T(8,128)(2,1)S(1)}, u32[]{:S(2)}, u32[]{:S(2)}) collective-permute-start(bf16[264,256]{1,0:T(8,128)(2,1)S(1)} %get-tuple-element.17), channel_id=1, source_target_pairs={{0,4},{4,0},{8,12},{12,8},{1,5},{5,1},{9,13},{13,9},{2,6},{6,2},{1... | collective-permute-start | bytes 405512 | tf_op jit(solution)/shard_map/ppermute | solution.py:336
  7.7 8.3 %collective-permute-start.2 = (bf16[136,256]{1,0:T(8,128)(2,1)S(1)}, bf16[136,256]{1,0:T(8,128)(2,1)S(1)}, u32[]{:S(2)}, u32[]{:S(2)}) collective-permute-start(bf16[136,256]{1,0:T(8,128)(2,1)S(1)} %get-tuple-element.18), channel_id=1, source_target_pairs={{0,12},{4,8},{8,4},{12,0},{1,13},{5,9},{9,5},{13,1},{2,14},{6,10},... | collective-permute-start | bytes 208904 | tf_op jit(solution)/shard_map/ppermute | solution.py:336
  7.7 9.6 %collective-permute-start.3 = (bf16[136,256]{1,0:T(8,128)(2,1)S(1)}, bf16[136,256]{1,0:T(8,128)(2,1)S(1)}, u32[]{:S(2)}, u32[]{:S(2)}) collective-permute-start(bf16[136,256]{1,0:T(8,128)(2,1)S(1)} %get-tuple-element.21), channel_id=1, source_target_pairs={{0,12},{4,8},{8,4},{12,0},{1,13},{5,9},{9,5},{13,1},{2,14},{6,10},... | collective-permute-start | bytes 208904 | tf_op jit(solution)/shard_map/ppermute | solution.py:336
  18.5 8.2 %collective-permute-start.4 = (s32[136,128]{1,0:T(8,128)S(1)}, s32[136,128]{1,0:T(8,128)S(1)}, u32[]{:S(2)}, u32[]{:S(2)}) collective-permute-start(s32[136,128]{1,0:T(8,128)S(1)} %get-tuple-element.25.refs_0_), channel_id=1, source_target_pairs={{0,4},{4,8},{8,12},{12,0},{1,5},{5,9},{9,13},{13,1},{2,6},{6,10},{... | collective-permute-start | bytes 208904 | tf_op jit(solution)/shard_map/ppermute | solution.py:384
  20.9 7.4 %collective-permute-start.5 = (s32[136,128]{1,0:T(8,128)S(1)}, s32[136,128]{1,0:T(8,128)S(1)}, u32[]{:S(2)}, u32[]{:S(2)}) collective-permute-start(s32[136,128]{1,0:T(8,128)S(1)} %get-tuple-element.25.refs_0_), channel_id=1, source_target_pairs={{0,8},{4,12},{8,0},{12,4},{1,9},{5,13},{9,1},{13,5},{2,10},{6,14},... | collective-permute-start | bytes 208904 | tf_op jit(solution)/shard_map/ppermute | solution.py:384
  22.6 5.7 %collective-permute-start.6 = (s32[136,128]{1,0:T(8,128)S(1)}, s32[136,128]{1,0:T(8,128)S(1)}, u32[]{:S(2)}, u32[]{:S(2)}) collective-permute-start(s32[136,128]{1,0:T(8,128)S(1)} %get-tuple-element.25.refs_0_), channel_id=1, source_target_pairs={{0,12},{4,0},{8,4},{12,8},{1,13},{5,1},{9,5},{13,9},{2,14},{6,2},{... | collective-permute-start | bytes 208904 | tf_op jit(solution)/shard_map/ppermute | solution.py:384

commit v5 on v4

--- a/solution.py
+++ b/solution.py
@@ -189,7 +189,7 @@
     weighted = jnp.concatenate(weighted, axis=0)
     largest = jnp.max(jnp.abs(weighted), axis=1, keepdims=True)
     level = jnp.ceil(jnp.log2(jnp.maximum(largest, SMALLEST)) * LEVELS)
-    codes = jnp.floor(weighted * (CODE_MAX / jnp.exp2(level / LEVELS)) + 0.5)
+    codes = jnp.floor(weighted * (CODE_MAX * jnp.exp2(level * (-1.0 / LEVELS))) + 0.5)
     codes = jnp.clip(codes, -CODE_MAX, CODE_MAX).astype(jnp.int32)
     stat_lane = lax.broadcasted_iota(jnp.int32, weighted.shape, 1)
     stats = jnp.zeros(weighted.shape, jnp.float32)
@@ -308,30 +308,32 @@
     distances = [0] + sorted(range(1, shards), key=lambda k: (k & (k - 1), -k))
     every = tuple(range(req_local))
     plan = [(k, every) for k in distances[:-1]] + [(distances[-1], (r,)) for r in every]
-    packed = pl.pallas_call(
-        functools.partial(pack_kernel, shards, capacity, kept_dev, req_local, plan),
-        out_shape=[
-            jax.ShapeDtypeStruct((len(m) * head_local * capacity + pairs, width), jnp.bfloat16)
-            for _, m in plan
-        ],
-        in_specs=[anywhere] * 3,
-        out_specs=[vmem] * len(plan),
-        scratch_shapes=[
-            pltpu.VMEM((pairs, evict_dev, width), jnp.bfloat16),
-            pltpu.VMEM((pairs, evict_dev), jnp.bfloat16),
-            pltpu.VMEM((pairs, evict_dev), jnp.int32),
-            pltpu.SemaphoreType.DMA((3,)),
-        ],
-        compiler_params=params,
-        name="pack",
-    )(
-        in_hbm(evicted.reshape(pairs, evict_dev, width)),
-        in_hbm(merge_weight.reshape(pairs, evict_dev)),
-        in_hbm(targets.reshape(pairs, evict_dev)),
-    )
-
-    messages = [packed[0]]
-    for (k, _), message in zip(plan[1:], packed[1:]):
+    def pack(plan):
+        return pl.pallas_call(
+            functools.partial(pack_kernel, shards, capacity, kept_dev, req_local, plan),
+            out_shape=[
+                jax.ShapeDtypeStruct((len(m) * head_local * capacity + pairs, width), jnp.bfloat16)
+                for _, m in plan
+            ],
+            in_specs=[anywhere] * 3,
+            out_specs=[vmem] * len(plan),
+            scratch_shapes=[
+                pltpu.VMEM((pairs, evict_dev, width), jnp.bfloat16),
+                pltpu.VMEM((pairs, evict_dev), jnp.bfloat16),
+                pltpu.VMEM((pairs, evict_dev), jnp.int32),
+                pltpu.SemaphoreType.DMA((3,)),
+            ],
+            compiler_params=params,
+            name="pack",
+        )(
+            in_hbm(evicted.reshape(pairs, evict_dev, width)),
+            in_hbm(merge_weight.reshape(pairs, evict_dev)),
+            in_hbm(targets.reshape(pairs, evict_dev)),
+        )
+
+    own, packed = pack(plan[:1]), pack(plan[1:])
+    messages = list(own)
+    for (k, _), message in zip(plan[1:], packed):
         pairing = [(i, at_distance(i, k, shards)) for i in range(shards)]
         messages.append(lax.ppermute(message, "seq", pairing))
 

time: 29.6 us -> 29.7 us (level)
  Pallas kernels: 7.46 us -> 8.86 us
  waiting for transfers between devices: 2.57 us -> 1.6 us
  starting transfers between devices: 16.4 us -> 16 us
    pallas_call x1 -> x2, Pallas kernels: 1.41 us -> 2.83 us  [pack(): pl.pallas_call(functools.partial(pack_kernel, shards, capacity, kept_dev,...]
    ppermute x4, waiting for transfers between devices: 0.98 us -> 0.01 us  [body(): messages.append(lax.ppermute(message, 'seq', pairing))]
    ppermute x3, starting transfers between devices: 6.9 us -> 6.45 us  [body(): partials.append(lax.ppermute(partial, 'seq', pairing))]
  transfers between devices with their start and end apart: 7 -> 7, of which waited for: 2 -> 1; matrix products, arithmetic and copies ran while one was open for 8% -> 8% of each run, Pallas kernels for 13% -> 18%
where the time goes in v5:
time: 29.7 us; the launch traced here: 29.4 us
  starting transfers between devices  16 us (54%)
  Pallas kernels  8.86 us (30%)
  local copies, waits for them, and re-layouts  1.83 us (6%)
  waiting for transfers between devices  1.6 us (5%)
  between operations  0.73 us (2%)
  matrix products  0.37 us (1%)
    ppermute x4, starting transfers between devices, body(): messages.append(lax.ppermute(message, 'seq', pairing))  9.5 us
    ppermute x3, starting transfers between devices, body(): partials.append(lax.ppermute(partial, 'seq', pairing))  6.45 us
    pallas_call x2, Pallas kernels, pack(): pl.pallas_call(functools.partial(pack_kernel, shards, capacity, kept_dev,...  2.83 us
    pallas_call x2, Pallas kernels, body(): pl.pallas_call(functools.partial(merge_kernel, shards, capacity, req_loca...  2.42 us
    ppermute x3, waiting for transfers between devices, body(): partials.append(lax.ppermute(partial, 'seq', pairing))  1.59 us
    pallas_call x1, Pallas kernels, body(): pl.pallas_call(load_kernel, out_shape=[block] * req_local, in_specs=[anyw...  1.39 us
    pallas_call x1, Pallas kernels, body(): pl.pallas_call(store_kernel, out_shape=pltpu.HBM((pairs, kept_dev, width)...  1.15 us
    pallas_call x1, Pallas kernels, body(): pl.pallas_call(functools.partial(combine_kernel, shards, head_local, kept...  1.07 us
  transfers between devices with their start and end apart: 7, of which 1 were waited for; matrix products, arithmetic and copies ran while one was open for 8% of the time, Pallas kernels for 18%

profile of v5, /device:TPU:0, one launch (start us, length us, event | category | flops | bytes accessed | tf_op | source)
XLA Modules:
  0.0 29.4 jit_solution(11937363199146214957)
XLA Ops:
  0.6 1.4 %pack.3 = (bf16[264,256]{1,0:T(8,128)(2,1)S(1)}, bf16[264,256]{1,0:T(8,128)(2,1)S(1)}, bf16[136,256]{1,0:T(8,128)(2,1)S(1)}, bf16[136,256]{1,0:T(8,128)(2,1)S(1)}) custom-call(bf16[8,64,256]{2,1,0:T(8,128)(2,1)} %bitcast.19, bf16[8,64]{1,0:T(8,128)(2,1)} %bitcast.27, s32[8,64]{1,0:T(8,128)} %bitcast.24), custom_call_target="tpu_custom_call" | custom-call | tf_op jit(solution)/shard_map/pack/pallas_call | solution.py:312
  2.1 4.1 %collective-permute-start = (bf16[264,256]{1,0:T(8,128)(2,1)S(1)}, bf16[264,256]{1,0:T(8,128)(2,1)S(1)}, u32[]{:S(2)}, u32[]{:S(2)}) collective-permute-start(bf16[264,256]{1,0:T(8,128)(2,1)S(1)} %get-tuple-element.14), channel_id=1, source_target_pairs={{0,8},{4,12},{8,0},{12,4},{1,9},{5,13},{9,1},{13,5},{2,10},{6,14},... | collective-permute-start | bytes 405512 | tf_op jit(solution)/shard_map/ppermute | solution.py:338
  6.2 1.6 %collective-permute-start.1 = (bf16[264,256]{1,0:T(8,128)(2,1)S(1)}, bf16[264,256]{1,0:T(8,128)(2,1)S(1)}, u32[]{:S(2)}, u32[]{:S(2)}) collective-permute-start(bf16[264,256]{1,0:T(8,128)(2,1)S(1)} %get-tuple-element.15), channel_id=1, source_target_pairs={{0,4},{4,0},{8,12},{12,8},{1,5},{5,1},{9,13},{13,9},{2,6},{6,2},{1... | collective-permute-start | bytes 405512 | tf_op jit(solution)/shard_map/ppermute | solution.py:338
  7.7 0.0 collective-permute-start.2
  7.7 3.8 %collective-permute-start.3 = (bf16[136,256]{1,0:T(8,128)(2,1)S(1)}, bf16[136,256]{1,0:T(8,128)(2,1)S(1)}, u32[]{:S(2)}, u32[]{:S(2)}) collective-permute-start(bf16[136,256]{1,0:T(8,128)(2,1)S(1)} %get-tuple-element.19), channel_id=1, source_target_pairs={{0,12},{4,8},{8,4},{12,0},{1,13},{5,9},{9,5},{13,1},{2,14},{6,10},... | collective-permute-start | bytes 208904 | tf_op jit(solution)/shard_map/ppermute | solution.py:338
  11.6 0.9 %copy.11 = bf16[4,2,4,8,128]{4,3,0,2,1:T(8,128)(2,1)S(1)} copy(bf16[4,2,4,8,128]{4,3,2,1,0:T(8,128)(2,1)} %bitcast.21) | data formatting | bytes 131072 | tf_op jit(solution)/shard_map/reshape | solution.py:340
  12.4 0.7 %copy.14 = bf16[2,4,4,256]{3,2,1,0:T(4,128)(2,1)S(1)} copy(bf16[2,4,4,256]{3,1,0,2:T(4,128)(2,1)} %bitcast.26) | data formatting | bytes 32768 | tf_op jit(solution)/shard_map/transpose | solution.py:342
  13.2 0.2 fusion.8
  13.3 0.2 fusion.3
  13.5 1.4 %pack.2.refs_3_ = bf16[264,256]{1,0:T(8,128)(2,1)S(1)} custom-call(bf16[8,64,256]{2,1,0:T(8,128)(2,1)} %bitcast.20, bf16[8,64]{1,0:T(8,128)(2,1)} %bitcast.28, s32[8,64]{1,0:T(8,128)} %bitcast.25), custom_call_target="tpu_custom_call" | custom-call | tf_op jit(solution)/shard_map/pack/pallas_call | solution.py:312
  15.0 0.1 reshape.81.refs_4_
  15.0 1.4 %stage.1 = (bf16[4,384,256]{2,1,0:T(8,128)(2,1)S(1)}, bf16[4,384,256]{2,1,0:T(8,128)(2,1)S(1)}) custom-call(bf16[8,384,256]{2,1,0:T(8,128)(2,1)} %bitcast.17), custom_call_target="tpu_custom_call" | custom-call | tf_op jit(solution)/shard_map/stage/pallas_call | solution.py:349
  16.4 0.1 copy.12.refs_2_
  16.5 0.0 collective-permute-done.2.refs_6_
  16.5 0.0 collective-permute-done.refs_4_
  16.5 1.2 %merge.2 = (bf16[4,384,256]{2,1,0:T(8,128)(2,1)S(1)}, s32[128,128]{1,0:T(8,128)S(1)}, f32[128,128]{1,0:T(8,128)S(1)}) custom-call(bf16[4,384,256]{2,1,0:T(8,128)(2,1)S(1)} %get-tuple-element.13.refs_0_, bf16[8,32,128]{2,1,0:T(8,128)(2,1)S(1)} %bitcast.14, s32[2,1]{1,0:T(2,128)S(1)} %copy.12.refs_2_, ...), custom_call_target="tpu_custom_call", output_to_operand_aliasing={{0}: (0, {})} | custom-call | tf_op jit(solution)/shard_map/merge/pallas_call | solution.py:367
  17.8 1.2 %merge.3 = (bf16[4,384,256]{2,1,0:T(8,128)(2,1)S(1)}, s32[136,128]{1,0:T(8,128)S(1)}) custom-call(bf16[4,384,256]{2,1,0:T(8,128)(2,1)S(1)} %get-tuple-element.18.refs_0_, bf16[8,32,128]{2,1,0:T(8,128)(2,1)S(1)} %bitcast.15, s32[2,1]{1,0:T(2,128)S(1)} %copy.12.refs_2_, bf16[264,256]{1,0:T(8,128)(2,1)S(1)} %pack.2.refs_3_, ...), custom_call_target="tpu_custom_call", output_to_operand_aliasing={{0}: (0, {})} | custom-call | tf_op jit(solution)/shard_map/merge/pallas_call | solution.py:367
  19.0 1.9 %collective-permute-start.4 = (s32[136,128]{1,0:T(8,128)S(1)}, s32[136,128]{1,0:T(8,128)S(1)}, u32[]{:S(2)}, u32[]{:S(2)}) collective-permute-start(s32[136,128]{1,0:T(8,128)S(1)} %get-tuple-element.23.refs_0_), channel_id=1, source_target_pairs={{0,4},{4,8},{8,12},{12,0},{1,5},{5,9},{9,13},{13,1},{2,6},{6,10},{... | collective-permute-start | bytes 208904 | tf_op jit(solution)/shard_map/ppermute | solution.py:386
  20.9 1.7 %collective-permute-start.5 = (s32[136,128]{1,0:T(8,128)S(1)}, s32[136,128]{1,0:T(8,128)S(1)}, u32[]{:S(2)}, u32[]{:S(2)}) collective-permute-start(s32[136,128]{1,0:T(8,128)S(1)} %get-tuple-element.23.refs_0_), channel_id=1, source_target_pairs={{0,8},{4,12},{8,0},{12,4},{1,9},{5,13},{9,1},{13,5},{2,10},{6,14},... | collective-permute-start | bytes 208904 | tf_op jit(solution)/shard_map/ppermute | solution.py:386
  22.6 2.8 %collective-permute-start.6 = (s32[136,128]{1,0:T(8,128)S(1)}, s32[136,128]{1,0:T(8,128)S(1)}, u32[]{:S(2)}, u32[]{:S(2)}) collective-permute-start(s32[136,128]{1,0:T(8,128)S(1)} %get-tuple-element.23.refs_0_), channel_id=1, source_target_pairs={{0,12},{4,0},{8,4},{12,8},{1,13},{5,1},{9,5},{13,9},{2,14},{6,2},{... | collective-permute-start | bytes 208904 | tf_op jit(solution)/shard_map/ppermute | solution.py:386
  25.5 0.1 reshape.82.refs_5_
  25.5 1.2 %unstage.1 = bf16[8,384,256]{2,1,0:T(8,128)(2,1)} custom-call(bf16[4,384,256]{2,1,0:T(8,128)(2,1)S(1)} %get-tuple-element.17.refs_0_, bf16[4,384,256]{2,1,0:T(8,128)(2,1)S(1)} %get-tuple-element.22.refs_1_), custom_call_target="tpu_custom_call" | custom-call | tf_op jit(solution)/shard_map/unstage/pallas_call | solution.py:388
  26.7 1.6 %collective-permute-done.5.refs_2_ = s32[136,128]{1,0:T(8,128)S(1)} collective-permute-done((s32[136,128]{1,0:T(8,128)S(1)}, s32[136,128]{1,0:T(8,128)S(1)}, u32[]{:S(2)}, u32[]{:S(2)}) %collective-permute-start.5) | collective-permute-done | bytes 69664 | tf_op jit(solution)/shard_map/ppermute | solution.py:386
  28.3 1.1 %combine.1 = bf16[4,2,32,128]{3,2,1,0:T(8,128)(2,1)} custom-call(s32[136,128]{1,0:T(8,128)S(1)} %get-tuple-element.23.refs_0_, s32[136,128]{1,0:T(8,128)S(1)} %collective-permute-done.4.refs_1_, s32[136,128]{1,0:T(8,128)S(1)} %collective-permute-done.5.refs_2_, s32[136,128]{1,0:T(8,128)S(1)} %collective-permute-done.6.refs_3_, ...), custom_call_target="tpu_custom_call" | custom-call | tf_op jit(solution)/shard_map/combine/pallas_call | solution.py:398
  (9 shorter events, 0.0 us)
Async XLA Ops:
  0.6 15.8 %copy-start = (s32[2,1]{0,1:T(1,128)S(1)}, s32[2,1]{0,1:T(1,128)}, u32[]{:S(2)}) copy-start(s32[2,1]{0,1:T(1,128)} %param.11) | copy-start | bytes 28
  2.1 14.5 %collective-permute-start = (bf16[264,256]{1,0:T(8,128)(2,1)S(1)}, bf16[264,256]{1,0:T(8,128)(2,1)S(1)}, u32[]{:S(2)}, u32[]{:S(2)}) collective-permute-start(bf16[264,256]{1,0:T(8,128)(2,1)S(1)} %get-tuple-element.14), channel_id=1, source_target_pairs={{0,8},{4,12},{8,0},{12,4},{1,9},{5,13},{9,1},{13,5},{2,10},{6,14},... | collective-permute-start | bytes 405512 | tf_op jit(solution)/shard_map/ppermute | solution.py:338
  6.2 10.4 %collective-permute-start.1 = (bf16[264,256]{1,0:T(8,128)(2,1)S(1)}, bf16[264,256]{1,0:T(8,128)(2,1)S(1)}, u32[]{:S(2)}, u32[]{:S(2)}) collective-permute-start(bf16[264,256]{1,0:T(8,128)(2,1)S(1)} %get-tuple-element.15), channel_id=1, source_target_pairs={{0,4},{4,0},{8,12},{12,8},{1,5},{5,1},{9,13},{13,9},{2,6},{6,2},{1... | collective-permute-start | bytes 405512 | tf_op jit(solution)/shard_map/ppermute | solution.py:338
  7.7 8.8 %collective-permute-start.2 = (bf16[136,256]{1,0:T(8,128)(2,1)S(1)}, bf16[136,256]{1,0:T(8,128)(2,1)S(1)}, u32[]{:S(2)}, u32[]{:S(2)}) collective-permute-start(bf16[136,256]{1,0:T(8,128)(2,1)S(1)} %get-tuple-element.16), channel_id=1, source_target_pairs={{0,12},{4,8},{8,4},{12,0},{1,13},{5,9},{9,5},{13,1},{2,14},{6,10},... | collective-permute-start | bytes 208904 | tf_op jit(solution)/shard_map/ppermute | solution.py:338
  7.7 10.0 %collective-permute-start.3 = (bf16[136,256]{1,0:T(8,128)(2,1)S(1)}, bf16[136,256]{1,0:T(8,128)(2,1)S(1)}, u32[]{:S(2)}, u32[]{:S(2)}) collective-permute-start(bf16[136,256]{1,0:T(8,128)(2,1)S(1)} %get-tuple-element.19), channel_id=1, source_target_pairs={{0,12},{4,8},{8,4},{12,0},{1,13},{5,9},{9,5},{13,1},{2,14},{6,10},... | collective-permute-start | bytes 208904 | tf_op jit(solution)/shard_map/ppermute | solution.py:338
  19.0 7.7 %collective-permute-start.4 = (s32[136,128]{1,0:T(8,128)S(1)}, s32[136,128]{1,0:T(8,128)S(1)}, u32[]{:S(2)}, u32[]{:S(2)}) collective-permute-start(s32[136,128]{1,0:T(8,128)S(1)} %get-tuple-element.23.refs_0_), channel_id=1, source_target_pairs={{0,4},{4,8},{8,12},{12,0},{1,5},{5,9},{9,13},{13,1},{2,6},{6,10},{... | collective-permute-start | bytes 208904 | tf_op jit(solution)/shard_map/ppermute | solution.py:386
  20.9 7.4 %collective-permute-start.5 = (s32[136,128]{1,0:T(8,128)S(1)}, s32[136,128]{1,0:T(8,128)S(1)}, u32[]{:S(2)}, u32[]{:S(2)}) collective-permute-start(s32[136,128]{1,0:T(8,128)S(1)} %get-tuple-element.23.refs_0_), channel_id=1, source_target_pairs={{0,8},{4,12},{8,0},{12,4},{1,9},{5,13},{9,1},{13,5},{2,10},{6,14},... | collective-permute-start | bytes 208904 | tf_op jit(solution)/shard_map/ppermute | solution.py:386
  22.6 5.7 %collective-permute-start.6 = (s32[136,128]{1,0:T(8,128)S(1)}, s32[136,128]{1,0:T(8,128)S(1)}, u32[]{:S(2)}, u32[]{:S(2)}) collective-permute-start(s32[136,128]{1,0:T(8,128)S(1)} %get-tuple-element.23.refs_0_), channel_id=1, source_target_pairs={{0,12},{4,0},{8,4},{12,8},{1,13},{5,1},{9,5},{13,9},{2,14},{6,2},{... | collective-permute-start | bytes 208904 | tf_op jit(solution)/shard_map/ppermute | solution.py:386
